TPU v7x, 32 devices: a whole 2x2x4 slice. The times are simulated.
32 devices in a mesh: lon: 8 (over y, x, core), lat: 4 (over z).
Axes of the slice: x: 2, y: 2, z: 4, core: 2. Of those that a mesh axis runs over, the one named last changes fastest.
Arguments:
- tracer: float32 [8, 512, 2048], P(None, 'lat', 'lon'), may hold values from -8 to 8
- courant: float32 [8, 512, 2048], P(None, 'lat', 'lon'), may hold values from 0.25 to 10240
- hop_counts: int32 [512], P('lat'), may hold values from 0 to 7, as said below
- row_area: float32 [512], P('lat'), may hold values from 1 to 10
Outputs:
- updated: float32 [8, 512, 2048], P(None, 'lat', 'lon')
- dateline_flux: float32 [8], replicated
Inputs may be any that keep to these rules, and one draw needn't show every extreme that they name: `hop_counts`: only the first 8 and the last 8 latitude rows may have counts above 0.
All inputs are finite; a program needn't handle non-finite values.
Results may differ from a plain program's by a relative error of at most 0.0003.
Values sent between devices are 32-bit elements; how exact they have to be, the bound alone decides.
A program may use at most 64 MiB of HBM per device.

v0:
```python
import jax
import jax.numpy as jnp
from jax import lax
from jax.sharding import PartitionSpec as P

STOPS = 7


def from_behind(array, axis, by):
    devices = lax.axis_size(axis)
    return lax.ppermute(array, axis, [(i, (i + by) % devices) for i in range(devices)])


def prefix(part, axis, combine, identity):
    place = lax.axis_index(axis)
    gathered = jax.tree.map(lambda a: lax.all_gather(a, axis), part)
    state = jax.tree.map(lambda a, e: jnp.zeros_like(a) + jnp.asarray(e, a.dtype), part, identity)

    def one(hop, state):
        return combine(
            state, jax.tree.map(lambda a: lax.dynamic_index_in_dim(a, hop, 0, False), gathered)
        )

    return lax.fori_loop(0, place, one, state)


def broadcast(block, axis, source):
    block = jnp.where(lax.axis_index(axis) == source, block, jnp.zeros_like(block))
    return lax.psum(block, axis)


def compose(earlier, latter):
    return (earlier[0] * latter[0], latter[0] * earlier[1] + latter[1])


def hop_slabs(slab_rows, counts):
    for bit_index in range(STOPS.bit_length()):
        arrived = from_behind(slab_rows, "lon", 1 << bit_index)
        chosen = jnp.right_shift(counts, bit_index) % 2 == 1
        slab_rows = jnp.where(chosen[None, :, None], arrived, slab_rows)
    return slab_rows


def within_block(factors, source):
    growth = factors
    offset = factors * source
    length = factors.shape[-1]
    stride = 1
    while stride < length:
        lead_growth = jnp.concatenate(
            [jnp.ones_like(growth[..., :stride]), growth[..., :-stride]], axis=-1
        )
        lead_offset = jnp.concatenate(
            [jnp.zeros_like(offset[..., :stride]), offset[..., :-stride]], axis=-1
        )
        offset = growth * lead_offset + offset
        growth = growth * lead_growth
        stride = stride * 2
    return (growth, offset)


def body(tracer, courant, hop_counts, row_area):
    source = hop_slabs(tracer, hop_counts)
    factors = courant / (1.0 + courant)
    growth, offset = within_block(factors, source)
    own_map = (growth[..., -1], offset[..., -1])
    identity = (jnp.ones_like(own_map[0]), jnp.zeros_like(own_map[1]))
    prior_growth, prior_offset = prefix(own_map, "lon", compose, identity)
    whole_map = compose((prior_growth, prior_offset), own_map)
    stacked = broadcast(jnp.stack(whole_map), "lon", lax.axis_size("lon") - 1)
    loop_growth = stacked[0]
    loop_offset = stacked[1]
    wrap = loop_offset / (1.0 - loop_growth)
    inflow = prior_growth * wrap + prior_offset
    flux = growth * inflow[..., None] + offset
    before = jnp.concatenate([inflow[..., None], flux[..., :-1]], axis=-1)
    updated = (source + before) / (1.0 + courant)
    weighted = jnp.sum(row_area[None, :] * wrap, axis=1)
    weighted_sum, area_sum = lax.psum((weighted, jnp.sum(row_area)), "lat")
    return (updated, weighted_sum / area_sum)


def solution(mesh):
    return jax.shard_map(
        body,
        mesh=mesh,
        in_specs=(P(None, "lat", "lon"), P(None, "lat", "lon"), P("lat"), P("lat")),
        out_specs=(P(None, "lat", "lon"), P()),
        check_vma=False,
    )
```

profile of v0, /device:TPU:0, one launch (start us, length us, event | category | flops | bytes accessed | tf_op | source)
XLA Modules:
  0.0 118.5 jit_solution(400795643414627318)
XLA Ops:
  0.6 1.7 %copy.24 = f32[8,128,256]{1,0,2:T(8,128)S(1)} copy(f32[8,128,256]{2,1,0:T(8,128)} %param.6) | data formatting | bytes 2097152 | tf_op args[0]
  2.3 0.5 collective-permute-start
  2.8 15.3 %collective-permute-done = f32[8,128,256]{1,0,2:T(8,128)S(1)} collective-permute-done((f32[8,128,256]{1,0,2:T(8,128)S(1)}, f32[8,128,256]{1,0,2:T(8,128)S(1)}, u32[]{:S(2)}, u32[]{:S(2)}) %collective-permute-start) | collective-permute-done | bytes 1048608 | tf_op jit(solution)/shard_map/ppermute | solution.py:11
  18.2 0.1 broadcast_select_fusion
  18.3 1.4 %collective-permute-start.1 = (f32[8,128,256]{1,0,2:T(8,128)S(1)}, f32[8,128,256]{1,0,2:T(8,128)S(1)}, u32[]{:S(2)}, u32[]{:S(2)}) collective-permute-start(f32[8,128,256]{1,0,2:T(8,128)S(1)} %broadcast_select_fusion), channel_id=1, source_target_pairs={{0,8},{4,12},{8,16},{12,20},{16,24},{20,28},{24,0},{28,4},{1,9},{5... | collective-permute-start | bytes 3145736 | tf_op jit(solution)/shard_map/ppermute | solution.py:11
  19.7 23.6 %collective-permute-done.1 = f32[8,128,256]{1,0,2:T(8,128)S(1)} collective-permute-done((f32[8,128,256]{1,0,2:T(8,128)S(1)}, f32[8,128,256]{1,0,2:T(8,128)S(1)}, u32[]{:S(2)}, u32[]{:S(2)}) %collective-permute-start.1) | collective-permute-done | bytes 1048608 | tf_op jit(solution)/shard_map/ppermute | solution.py:11
  43.4 1.6 %collective-permute-start.2 = (f32[8,128,256]{1,0,2:T(8,128)S(1)}, f32[8,128,256]{1,0,2:T(8,128)S(1)}, u32[]{:S(2)}, u32[]{:S(2)}) collective-permute-start(f32[8,128,256]{1,0,2:T(8,128)S(1)} %broadcast_select_fusion.1), channel_id=1, source_target_pairs={{0,16},{4,20},{8,24},{12,28},{16,0},{20,4},{24,8},{28,12},{1,17},{... | collective-permute-start | bytes 3145736 | tf_op jit(solution)/shard_map/ppermute | solution.py:11
  45.0 1.6 %copy.27 = f32[8,128,256]{1,0,2:T(8,128)S(1)} copy(f32[8,128,256]{2,1,0:T(8,128)} %param.7) | data formatting | bytes 2097152 | tf_op args[1]
  46.7 0.6 copy-done.3
  47.3 0.6 reduce_sum.19
  47.9 18.7 %collective-permute-done.2 = f32[8,128,256]{1,0,2:T(8,128)S(1)} collective-permute-done((f32[8,128,256]{1,0,2:T(8,128)S(1)}, f32[8,128,256]{1,0,2:T(8,128)S(1)}, u32[]{:S(2)}, u32[]{:S(2)}) %collective-permute-start.2) | collective-permute-done | bytes 1048608 | tf_op jit(solution)/shard_map/ppermute | solution.py:11
  66.6 0.2 add_divide_fusion.1
  66.8 0.8 copy-done.1
  67.6 0.3 multiply_add_fusion.7
  68.0 0.3 multiply_add_fusion.6
  68.5 0.3 multiply_add_fusion.5
  68.9 0.2 multiply_add_fusion.4
  69.3 0.2 multiply_add_fusion.3
  69.7 0.2 multiply_add_fusion.2
  70.0 0.2 multiply_add_fusion.1
  70.3 0.2 multiply_add_fusion
  70.7 8.3 %all-gather = f32[64,128,1]{1,0,2:T(8,128)S(1)} all-gather(f32[8,128,1]{1,0,2:T(8,128)S(1)} %slice.92), channel_id=2, replica_groups=mesh['lon'=8,'lat'=4] {'lon'}, dimensions={0}, use_global_device_ids=true | all-gather | bytes 36864 | tf_op jit(solution)/shard_map/all_gather | solution.py:16
  79.0 8.8 %all-gather.1 = f32[64,128,1]{1,0,2:T(8,128)S(1)} all-gather(f32[8,128,1]{1,0,2:T(8,128)S(1)} %slice.101), channel_id=3, replica_groups=mesh['lon'=8,'lat'=4] {'lon'}, dimensions={0}, use_global_device_ids=true | all-gather | bytes 36864 | tf_op jit(solution)/shard_map/all_gather | solution.py:16
  87.8 0.7 fusion.4
  88.5 13.7 %psum.21 = f32[2,8,128]{2,1,0:T(8,128)S(1)} all-reduce(f32[2,8,128]{2,1,0:T(8,128)S(1)} %maximum_select_fusion), channel_id=1, replica_groups=mesh['lon'=8,'lat'=4] {'lon'}, use_global_device_ids=true, to_apply=%region_2.3 | all-reduce | flops 2048 | bytes 16384 | tf_op jit(solution)/shard_map/psum | solution.py:29
  102.2 0.1 multiply_reduce_fusion
  102.3 1.4 %slice_add_fusion = f32[8,128,255]{1,0,2:T(8,128)S(1)} fusion(f32[8,128,256]{1,0,2:T(8,128)} %copy-done, f32[8,128,256]{1,0,2:T(8,128)S(1)} %pad_multiply_fusion, f32[8,128]{1,0:T(8,128)S(1)} %get-tuple-element.75), kind=kLoop, calls=%fused_computation.22 | loop fusion | flops 522240 | bytes 3137536 | tf_op jit(solution)/shard_map/add | solution.py:75
  103.7 0.1 copy-done.2
  103.9 0.3 add_divide_fusion
  104.1 1.4 %copy.28 = f32[8,128,256]{2,1,0:T(8,128)} copy(f32[8,128,256]{1,0,2:T(8,128)S(1)} %add_divide_fusion) | data formatting | bytes 2097152
  105.5 11.8 %all-reduce.16 = (f32[8]{0:T(128)S(1)}, f32[]{:T(128)}) all-reduce(f32[8]{0:T(128)S(1)} %get-tuple-element.74, f32[]{:T(128)} %reduce_sum.19), channel_id=1, replica_groups=mesh['lon'=8,'lat'=4] {'lat'}, use_global_device_ids=true, to_apply=%region_4.5 | all-reduce | flops 9 | bytes 72 | tf_op jit(solution)/shard_map/psum | solution.py:79
  117.3 1.1 broadcast_divide_fusion
  (32 shorter events, 1.2 us)
Async XLA Ops:
  0.6 2.2 %copy-start.4 = (s32[128]{0:T(128)S(1)}, s32[128]{0:T(128)}, u32[]{:S(2)}) copy-start(s32[128]{0:T(128)} %param.8) | copy-start | bytes 1540
  2.3 15.9 %collective-permute-start = (f32[8,128,256]{1,0,2:T(8,128)S(1)}, f32[8,128,256]{1,0,2:T(8,128)S(1)}, u32[]{:S(2)}, u32[]{:S(2)}) collective-permute-start(f32[8,128,256]{1,0,2:T(8,128)S(1)} %copy.24), channel_id=1, source_target_pairs={{0,4},{4,8},{8,12},{12,16},{16,20},{20,24},{24,28},{28,0},{1,5},{5... | collective-permute-start | bytes 3145736 | tf_op jit(solution)/shard_map/ppermute | solution.py:11
  18.3 25.0 %collective-permute-start.1 = (f32[8,128,256]{1,0,2:T(8,128)S(1)}, f32[8,128,256]{1,0,2:T(8,128)S(1)}, u32[]{:S(2)}, u32[]{:S(2)}) collective-permute-start(f32[8,128,256]{1,0,2:T(8,128)S(1)} %broadcast_select_fusion), channel_id=1, source_target_pairs={{0,8},{4,12},{8,16},{12,20},{16,24},{20,28},{24,0},{28,4},{1,9},{5... | collective-permute-start | bytes 3145736 | tf_op jit(solution)/shard_map/ppermute | solution.py:11
  43.4 23.2 %collective-permute-start.2 = (f32[8,128,256]{1,0,2:T(8,128)S(1)}, f32[8,128,256]{1,0,2:T(8,128)S(1)}, u32[]{:S(2)}, u32[]{:S(2)}) collective-permute-start(f32[8,128,256]{1,0,2:T(8,128)S(1)} %broadcast_select_fusion.1), channel_id=1, source_target_pairs={{0,16},{4,20},{8,24},{12,28},{16,0},{20,4},{24,8},{28,12},{1,17},{... | collective-permute-start | bytes 3145736 | tf_op jit(solution)/shard_map/ppermute | solution.py:11
  46.6 0.7 copy-start.3
  66.6 1.0 copy-start.1
  70.5 8.5 %copy-start = (f32[8,128,256]{1,0,2:T(8,128)}, f32[8,128,256]{1,0,2:T(8,128)S(1)}, u32[]{:S(2)}) copy-start(f32[8,128,256]{1,0,2:T(8,128)S(1)} %get-tuple-element.54) | copy-start | bytes 3145732
  102.3 1.5 %copy-start.2 = (f32[8,128,256]{1,0,2:T(8,128)S(1)}, f32[8,128,256]{1,0,2:T(8,128)}, u32[]{:S(2)}) copy-start(f32[8,128,256]{1,0,2:T(8,128)} %copy-done.1) | copy-start | bytes 3145732
where the time goes:
time: 119 us; the launch traced here: 118 us
  waiting for transfers between devices  57.6 us (48%)
  blocking collectives  42.7 us (36%)
  local copies, waits for them, and re-layouts  7.21 us (6%)
  other arithmetic  6.63 us (6%)
  starting transfers between devices  3.49 us (3%)
    ppermute x3, waiting for transfers between devices, from_behind(): lax.ppermute(array, axis, [(i, (i + by) % devices) for i in range(devices)])  57.6 us
    all_gather x2, blocking collectives, prefix(): gathered = jax.tree.map(lambda a: lax.all_gather(a, axis), part)  17.1 us
    psum x1, blocking collectives, broadcast(): return lax.psum(block, axis)  13.7 us
    psum x1, blocking collectives, body(): weighted_sum, area_sum = lax.psum((weighted, jnp.sum(row_area)), 'lat')  11.8 us
    unnamed x13, local copies, waits for them, and re-layouts  6.23 us
    ppermute x3, starting transfers between devices, from_behind(): lax.ppermute(array, axis, [(i, (i + by) % devices) for i in range(devices)])  3.49 us
  transfers between devices with their start and end apart: 3, of which 3 were waited for; matrix products, arithmetic and copies ran while one was open for 2% of the time, Pallas kernels for 0%

commit v1 on v0

v1 whole, which is shorter than its diff:
```python
import functools

import jax
import jax.numpy as jnp
from jax import lax
from jax.experimental import pallas as pl
from jax.experimental.pallas import tpu as pltpu
from jax.sharding import PartitionSpec as P

POLAR = 8
STOPS = 7
LANES = 128
CHUNK = 32


def lane_index(shape):
    return lax.broadcasted_iota(jnp.int32, shape, len(shape) - 1)


def scan_lanes(growth, offset):
    lane = lane_index(growth.shape)
    stride = 1
    while stride < LANES:
        inside = lane >= stride
        lead_growth = pltpu.roll(growth, stride, 1)
        lead_offset = pltpu.roll(offset, stride, 1)
        offset = jnp.where(inside, growth * lead_offset + offset, offset)
        growth = jnp.where(inside, growth * lead_growth, growth)
        stride *= 2
    return growth, offset


def solve_block(courants, sources):
    out, end = [], None
    for courant, source in zip(courants, sources):
        above = 1.0 + courant
        shared = 1.0 / (courant * above)
        ratio = 1.0 - shared * courant
        inverse = shared * above
        growth, offset = scan_lanes(ratio, ratio * source)
        if end is not None:
            offset = growth * end[1] + offset
            growth = growth * end[0]
        end = (
            jnp.broadcast_to(growth[:, LANES - 1 :], growth.shape),
            jnp.broadcast_to(offset[:, LANES - 1 :], offset.shape),
        )
        out.append((growth * inverse, offset * inverse))
    return out, end


def kernel(
    n, z, tracer, courant, hops, area, updated, dateline,
    trv, cov, ends, maps, pt, pc, pu, back, part,
    in_sem, own_sem, p_send, p_recv, m_send, m_recv, b_send, b_recv, d_send, d_recv,
):
    levels, rows, cells = trv.shape
    halves = cells // LANES
    me = lax.axis_index("lon")
    lat = lax.axis_index("lat")
    polar = (lat == 0) | (lat == z - 1)
    row0 = pl.multiple_of(jnp.where(lat == 0, 0, rows - POLAR), POLAR)
    slab = pl.ds(row0, POLAR)

    def ahead(k):
        return lax.rem(me + k, n)

    def behind(k):
        return lax.rem(me + n - k, n)

    def is_worker(device, work):
        if n == levels:
            work()
        else:
            pl.when(device < levels)(work)

    barrier = pltpu.get_barrier_semaphore()
    for k in range(1, n):
        pl.semaphore_signal(barrier, inc=1, device_id={"lon": ahead(k)}, device_id_type=pl.DeviceIdType.MESH)
    for k in range(1, z):
        pl.semaphore_signal(
            barrier, inc=1, device_id={"lat": lax.rem(lat + k, z)}, device_id_type=pl.DeviceIdType.MESH
        )

    def load(l):
        return (
            pltpu.make_async_copy(tracer.at[l], trv.at[l], in_sem.at[0, l]),
            pltpu.make_async_copy(courant.at[l], cov.at[l], in_sem.at[1, l]),
        )

    for l in range(levels):
        for copy in load(l):
            copy.start()

    def remote(source, target, send, recv, k, axis="lon"):
        place = ahead(k) if axis == "lon" else lax.rem(lat + k, z)
        return pltpu.make_async_remote_copy(
            src_ref=source, dst_ref=target, send_sem=send, recv_sem=recv,
            device_id={axis: place}, device_id_type=pl.DeviceIdType.MESH,
        )

    def polar_out(k):
        level = lax.rem(ahead(k), levels)
        return (
            remote(courant.at[level, slab], pc.at[me], p_send.at[0, k], p_recv.at[0, k], k),
            remote(tracer.at[level, slab], pt.at[me], p_send.at[1, k], p_recv.at[1, k], k),
        )

    def polar_own():
        level = lax.rem(me, levels)
        return (
            pltpu.make_async_copy(courant.at[level, slab], pc.at[me], own_sem.at[0]),
            pltpu.make_async_copy(tracer.at[level, slab], pt.at[me], own_sem.at[1]),
        )

    pl.semaphore_wait(barrier, n + z - 2)

    @pl.when(polar)
    def _():
        for k in range(1, n):
            def send(k=k):
                for copy in polar_out(k):
                    copy.start()
            is_worker(ahead(k), send)

        def own():
            for copy in polar_own():
                copy.start()
        is_worker(me, own)

    @pl.loop(0, levels)
    def _(l):
        for copy in load(l):
            copy.wait()
        for first in range(0, rows, CHUNK):
            part_rows = pl.ds(first, CHUNK)
            columns = [pl.ds(h * LANES, LANES) for h in range(halves)]
            out, end = solve_block(
                [cov[l, part_rows, c] for c in columns], [trv[l, part_rows, c] for c in columns]
            )
            for c, (growth, offset) in zip(columns, out):
                cov[l, part_rows, c] = growth
                trv[l, part_rows, c] = offset
            lane = lane_index((CHUNK, LANES))
            held = jnp.where(lane == l, end[0], ends[part_rows, :])
            ends[part_rows, :] = jnp.where(lane == l + levels, end[1], held)

    maps[me] = jnp.transpose(ends[...])[: 2 * levels]

    def map_out(k):
        return remote(maps.at[me], maps.at[me], m_send.at[k], m_recv.at[k], k)

    for k in range(1, n):
        map_out(k).start()

    lane = lane_index((POLAR, LANES))
    sublane = lax.broadcasted_iota(jnp.int32, (POLAR, LANES), 0)

    def back_out(k):
        return remote(
            pu.at[ahead(k)], back.at[lax.rem(me, levels)], b_send.at[k], b_recv.at[k], k
        )

    def column(values):
        place = lane_index((POLAR, rows)) == lax.broadcasted_iota(jnp.int32, (POLAR, rows), 0) + row0
        return jnp.sum(jnp.where(place, jnp.broadcast_to(values, (POLAR, rows)), 0.0), axis=1, keepdims=True)

    def solve_polar():
        for k in range(1, n):
            for copy in polar_out(k):
                copy.wait_recv()
        for copy in polar_own():
            copy.wait()
        count = jnp.broadcast_to(column(hops[...].astype(jnp.float32)), (POLAR, LANES)).astype(jnp.int32)
        courants, sources = [], []
        for h in range(halves):
            c = pl.ds(h * LANES, LANES)
            blocks = [pt[s, :, c] for s in range(n)]
            for bit in range(STOPS.bit_length()):
                chosen = jnp.right_shift(count, bit) % 2 == 1
                blocks = [
                    jnp.where(chosen, blocks[(s - (1 << bit)) % n], blocks[s]) for s in range(n)
                ]
            sources.append(jnp.concatenate(blocks, axis=0))
            courants.append(jnp.concatenate([pc[s, :, c] for s in range(n)], axis=0))
        out, end = solve_block(courants, sources)
        growth = jnp.ones((POLAR, LANES), jnp.float32)
        offset = jnp.zeros((POLAR, LANES), jnp.float32)
        prior = []
        for s in range(n):
            prior.append((growth, offset))
            own = slice(s * POLAR, (s + 1) * POLAR)
            offset = end[0][own] * offset + end[1][own]
            growth = growth * end[0][own]
        wrap = offset / (1.0 - growth)
        weighted = jnp.sum(column(area[...]) * wrap, axis=0, keepdims=True)
        weighted = jnp.broadcast_to(weighted, (POLAR, LANES))
        for s in range(n):
            inflow = prior[s][0] * wrap + prior[s][1]
            own = slice(s * POLAR, (s + 1) * POLAR)
            for h, (g, o) in enumerate(out):
                c = pl.ds(h * LANES, LANES)
                pu[s, :POLAR, c] = g[own] * inflow + o[own]
                pu[s, POLAR:, c] = weighted
        for k in range(1, n):
            back_out(k).start()
        back[lax.rem(me, levels)] = pu[me]

    @pl.when(polar)
    def _():
        is_worker(me, solve_polar)

    for k in range(1, n):
        map_out(k).wait_recv()
    growth = jnp.ones((levels, rows), jnp.float32)
    offset = jnp.zeros((levels, rows), jnp.float32)
    prior_growth, prior_offset = growth, offset
    for s in range(n):
        here = s == me
        prior_growth = jnp.where(here, growth, prior_growth)
        prior_offset = jnp.where(here, offset, prior_offset)
        own = maps[s]
        offset = own[:levels] * offset + own[levels:]
        growth = growth * own[:levels]
    wrap = offset / (1.0 - growth)
    inflow = prior_growth * wrap + prior_offset
    spread = jnp.transpose(jnp.concatenate([inflow] * (LANES // levels), axis=0))

    areas = jnp.broadcast_to(area[...], (levels, rows))
    row = lane_index((levels, rows))
    masked = polar & (row >= row0) & (row < row0 + POLAR)
    part[lat, :levels] = jnp.where(masked, 0.0, areas * wrap)
    part[lat, levels:] = areas

    for l in range(levels):
        for first in range(0, rows, CHUNK):
            part_rows = pl.ds(first, CHUNK)
            level_inflow = jnp.broadcast_to(spread[first : first + CHUNK, l : l + 1], (CHUNK, LANES))
            for h in range(halves):
                c = pl.ds(h * LANES, LANES)
                updated[l, part_rows, c] = cov[l, part_rows, c] * level_inflow + trv[l, part_rows, c]

    def part_out(k):
        return remote(part.at[lat], part.at[lat], d_send.at[k], d_recv.at[k], k, "lat")

    @pl.when(polar)
    def _():
        for k in range(1, n):
            def receive(k=k):
                back_out(k).wait_recv()
            is_worker(behind(k), receive)
        total = jnp.zeros((levels, LANES), jnp.float32)
        sub = lax.broadcasted_iota(jnp.int32, (levels, LANES), 0)
        for l in range(levels):
            total = jnp.where(sub == l, back[l, POLAR : POLAR + 1, :LANES], total)
        first_lane = lane_index((levels, LANES)) == 0
        part[lat, :levels, :LANES] = part[lat, :levels, :LANES] + jnp.where(first_lane, total, 0.0)

    for k in range(1, z):
        part_out(k).start()

    @pl.when(polar)
    def _():
        for l in range(levels):
            updated[l, slab, :] = back[l, :POLAR, :]

    for k in range(1, z):
        part_out(k).wait_recv()
    total = part[0]
    for s in range(1, z):
        total = total + part[s]
    sums = jnp.sum(total, axis=1, keepdims=True)
    mean = jnp.broadcast_to(sums[:levels] / sums[levels:], (levels, LANES))
    diagonal = lax.broadcasted_iota(jnp.int32, (levels, LANES), 0) == lane_index((levels, LANES))
    dateline[...] = jnp.sum(jnp.where(diagonal, mean, 0.0), axis=0, keepdims=True)[:, :levels]

    for k in range(1, z):
        part_out(k).wait_send()
    for k in range(1, n):
        map_out(k).wait_send()

    @pl.when(polar)
    def _():
        for k in range(1, n):
            def sent(k=k):
                for copy in polar_out(k):
                    copy.wait_send()
            is_worker(ahead(k), sent)

        def returned():
            for k in range(1, n):
                back_out(k).wait_send()
        is_worker(me, returned)


def body(n, z, tracer, courant, hop_counts, row_area):
    levels, rows, cells = tracer.shape
    f32 = jnp.float32
    vmem = pl.BlockSpec(memory_space=pltpu.VMEM)
    hbm = pl.BlockSpec(memory_space=pl.ANY)
    dma = pltpu.SemaphoreType.DMA
    updated, dateline = pl.pallas_call(
        functools.partial(kernel, n, z),
        out_shape=(
            jax.ShapeDtypeStruct(tracer.shape, f32),
            jax.ShapeDtypeStruct((1, levels), f32),
        ),
        in_specs=[hbm, hbm, vmem, vmem],
        out_specs=(vmem, vmem),
        scratch_shapes=[
            pltpu.VMEM(tracer.shape, f32),
            pltpu.VMEM(tracer.shape, f32),
            pltpu.VMEM((rows, LANES), f32),
            pltpu.VMEM((n, 2 * levels, rows), f32),
            pltpu.VMEM((n, POLAR, cells), f32),
            pltpu.VMEM((n, POLAR, cells), f32),
            pltpu.VMEM((n, 2 * POLAR, cells), f32),
            pltpu.VMEM((levels, 2 * POLAR, cells), f32),
            pltpu.VMEM((z, 2 * levels, rows), f32),
            dma((2, levels)), dma((2,)),
            dma((2, n)), dma((2, n)),
            dma((n,)), dma((n,)),
            dma((n,)), dma((n,)),
            dma((z,)), dma((z,)),
        ],
        compiler_params=pltpu.CompilerParams(
            collective_id=0, has_side_effects=True, vmem_limit_bytes=16 * 1024 * 1024
        ),
        cost_estimate=pl.CostEstimate(
            flops=60 * tracer.size, bytes_accessed=12 * tracer.size, transcendentals=tracer.size
        ),
    )(tracer, courant, hop_counts.reshape(1, rows), row_area.reshape(1, rows))
    return updated, dateline.reshape(levels)


def solution(mesh):
    return jax.shard_map(
        functools.partial(body, mesh.shape["lon"], mesh.shape["lat"]),
        mesh=mesh,
        in_specs=(P(None, "lat", "lon"), P(None, "lat", "lon"), P("lat"), P("lat")),
        out_specs=(P(None, "lat", "lon"), P()),
        check_vma=False,
    )
```

time: 119 us -> 28.4 us (0.24)
  waiting for transfers between devices: 57.6 us -> 0 us
  blocking collectives: 42.7 us -> 0 us
  Pallas kernels: 0 us -> 22.9 us
  other arithmetic: 6.63 us -> 0 us
  starting transfers between devices: 3.49 us -> 0 us
  local copies, waits for them, and re-layouts: 7.21 us -> 4.59 us
    ppermute x3 -> x0, waiting for transfers between devices: 57.6 us -> none  [from_behind(): lax.ppermute(array, axis, [(i, (i + by) % devices) for i in range(devices)])]
    psum x2 -> x0, blocking collectives: 25.5 us -> none  [the longest x1 13.7 us: broadcast(): return lax.psum(block, axis)]
    pallas_call x0 -> x1, Pallas kernels: none -> 22.9 us  [body(): pl.pallas_call(functools.partial(kernel, n, z), out_shape=(jax.ShapeDtype...]
    all_gather x2 -> x0, blocking collectives: 17.1 us -> none  [prefix(): gathered = jax.tree.map(lambda a: lax.all_gather(a, axis), part)]
    ppermute x3 -> x0, starting transfers between devices: 3.49 us -> none  [from_behind(): lax.ppermute(array, axis, [(i, (i + by) % devices) for i in range(devices)])]
    add x9 -> x0, other arithmetic: 3.26 us -> none  [the longest x8 1.84 us: within_block(): offset = growth * lead_offset + offset]
    unnamed x13 -> x10, local copies, waits for them, and re-layouts: 6.23 us -> 4.59 us
    div x3 -> x0, other arithmetic: 1.61 us -> none  [the longest x1 1.15 us: body(): return (updated, weighted_sum / area_sum)]
  transfers between devices with their start and end apart: 3 -> 0, of which waited for: 3 -> 0; matrix products, arithmetic and copies ran while one was open for 2% -> 0% of each run, Pallas kernels for 0% -> 0%
where the time goes in v1:
time: 28.4 us; the launch traced here: 28.2 us
  Pallas kernels  22.9 us (81%)
  local copies, waits for them, and re-layouts  4.59 us (16%)
  between operations  0.66 us (2%)
    pallas_call x1, Pallas kernels, body(): pl.pallas_call(functools.partial(kernel, n, z), out_shape=(jax.ShapeDtype...  22.9 us
    unnamed x10, local copies, waits for them, and re-layouts  4.59 us

profile of v1, /device:TPU:0, one launch (start us, length us, event | category | flops | bytes accessed | tf_op | source)
XLA Modules:
  0.0 28.2 jit_solution(1520460721866448783)
XLA Ops:
  0.6 0.0 copy-start.2
  0.6 0.0 copy-start.3
  0.7 0.6 %copy-done.2 = s32[128]{0:T(128)S(1)} copy-done((s32[128]{0:T(128)S(1)}, s32[128]{0:T(128)}, u32[]{:S(2)}) %copy-start.2) | copy-done | bytes 536
  1.3 0.0 copy-done.3
  1.3 0.0 copy-start
  1.3 1.2 %copy-done = f32[8,128,256]{2,1,0:T(8,128)S(1)} copy-done((f32[8,128,256]{2,1,0:T(8,128)S(1)}, f32[8,128,256]{2,1,0:T(8,128)}, u32[]{:S(2)}) %copy-start) | copy-done | bytes 1048600
  2.5 0.0 copy-start.1
  2.5 1.2 %copy-done.1 = f32[8,128,256]{2,1,0:T(8,128)S(1)} copy-done((f32[8,128,256]{2,1,0:T(8,128)S(1)}, f32[8,128,256]{2,1,0:T(8,128)}, u32[]{:S(2)}) %copy-start.1) | copy-done | bytes 1048600
  3.8 22.9 %shard_map.59 = (f32[8,128,256]{2,1,0:T(8,128)S(1)}, f32[1,8]{1,0:T(1,128)S(1)}) custom-call(f32[8,128,256]{2,1,0:T(8,128)S(1)} %copy-done, f32[8,128,256]{2,1,0:T(8,128)S(1)} %copy-done.1, s32[1,128]{1,0:T(1,128)S(1)} %bitcast.3, f32[1,128]{1,0:T(1,128)S(1)} %bitcast.4), custom_call_target="tpu_custom_call" | custom-call | flops 15728640 | bytes 3145728 | tf_op jit(solution)/shard_map/pallas_call | solution.py:302
  26.7 1.0 %copy.8 = f32[8,128,256]{2,1,0:T(8,128)} copy(f32[8,128,256]{2,1,0:T(8,128)S(1)} %get-tuple-element.8) | data formatting | bytes 2097152
  27.7 0.5 %copy.9 = f32[8]{0:T(128)} copy(f32[8]{0:T(128)S(1)} %bitcast.5) | data formatting | bytes 64
Async XLA Ops:
  0.6 0.7 %copy-start.2 = (s32[128]{0:T(128)S(1)}, s32[128]{0:T(128)}, u32[]{:S(2)}) copy-start(s32[128]{0:T(128)} %param.6) | copy-start | bytes 1540
  0.6 0.7 %copy-start.3 = (f32[128]{0:T(128)S(1)}, f32[128]{0:T(128)}, u32[]{:S(2)}) copy-start(f32[128]{0:T(128)} %param.7) | copy-start | bytes 1540
  1.3 1.2 %copy-start = (f32[8,128,256]{2,1,0:T(8,128)S(1)}, f32[8,128,256]{2,1,0:T(8,128)}, u32[]{:S(2)}) copy-start(f32[8,128,256]{2,1,0:T(8,128)} %tracer.1) | copy-start | bytes 3145732
  2.5 1.2 %copy-start.1 = (f32[8,128,256]{2,1,0:T(8,128)S(1)}, f32[8,128,256]{2,1,0:T(8,128)}, u32[]{:S(2)}) copy-start(f32[8,128,256]{2,1,0:T(8,128)} %courant.1) | copy-start | bytes 3145732

commit v2 on v1

--- a/solution.py
+++ b/solution.py
@@ -10,7 +10,7 @@
 POLAR = 8
 STOPS = 7
 LANES = 128
-CHUNK = 32
+CHUNKS = 8
 
 
 def lane_index(shape):
@@ -50,9 +50,9 @@
 
 
 def kernel(
-    n, z, tracer, courant, hops, area, updated, dateline,
-    trv, cov, ends, maps, pt, pc, pu, back, part,
-    in_sem, own_sem, p_send, p_recv, m_send, m_recv, b_send, b_recv, d_send, d_recv,
+    n, z, tracer, courant, hops_in, area_in, updated, dateline,
+    trv, cov, st, ct, gs, os, maps, pt, pc, pu, back, part,
+    hops, area, small_sem, in_sem, own_sem, p_send, p_recv, m_send, m_recv, b_send, b_recv, d_send, d_recv,
 ):
     levels, rows, cells = trv.shape
     halves = cells // LANES
@@ -91,6 +91,12 @@
     for l in range(levels):
         for copy in load(l):
             copy.start()
+    small = (
+        pltpu.make_async_copy(hops_in, hops, small_sem.at[0]),
+        pltpu.make_async_copy(area_in, area, small_sem.at[1]),
+    )
+    for copy in small:
+        copy.start()
 
     def remote(source, target, send, recv, k, axis="lon"):
         place = ahead(k) if axis == "lon" else lax.rem(lat + k, z)
@@ -132,20 +138,49 @@
     def _(l):
         for copy in load(l):
             copy.wait()
-        for first in range(0, rows, CHUNK):
-            part_rows = pl.ds(first, CHUNK)
-            columns = [pl.ds(h * LANES, LANES) for h in range(halves)]
-            out, end = solve_block(
-                [cov[l, part_rows, c] for c in columns], [trv[l, part_rows, c] for c in columns]
-            )
-            for c, (growth, offset) in zip(columns, out):
-                cov[l, part_rows, c] = growth
-                trv[l, part_rows, c] = offset
-            lane = lane_index((CHUNK, LANES))
-            held = jnp.where(lane == l, end[0], ends[part_rows, :])
-            ends[part_rows, :] = jnp.where(lane == l + levels, end[1], held)
-
-    maps[me] = jnp.transpose(ends[...])[: 2 * levels]
+        for h in range(halves):
+            c = pl.ds(h * LANES, LANES)
+            ct[l, c, :] = jnp.transpose(cov[l, :, c])
+            st[l, c, :] = jnp.transpose(trv[l, :, c])
+
+    for copy in small:
+        copy.wait()
+    steps = cells // CHUNKS
+
+    def step(v, state):
+        growth, offset = state
+        cells_v = pl.ds(v, CHUNKS, stride=steps)
+        here, source = ct[:, cells_v, :], st[:, cells_v, :]
+        above = 1.0 + here
+        shared = 1.0 / (here * above)
+        ratio = 1.0 - shared * here
+        inverse = shared * above
+        growth = growth * ratio
+        offset = ratio * source + ratio * offset
+        gs[v] = growth * inverse
+        os[v] = offset * inverse
+        return growth, offset
+
+    shape = (levels, CHUNKS, rows)
+    growth, offset = lax.fori_loop(
+        0, steps, step, (jnp.ones(shape, jnp.float32), jnp.zeros(shape, jnp.float32)), unroll=4
+    )
+    sub = lax.broadcasted_iota(jnp.int32, (CHUNKS, rows), 0)
+    before = []
+    for l in range(levels):
+        g, o = growth[l], offset[l]
+        stride = 1
+        while stride < CHUNKS:
+            inside = sub >= stride
+            lead_g, lead_o = pltpu.roll(g, stride, 0), pltpu.roll(o, stride, 0)
+            o = jnp.where(inside, g * lead_o + o, o)
+            g = jnp.where(inside, g * lead_g, g)
+            stride *= 2
+        maps[me, l : l + 1, :] = g[CHUNKS - 1 :]
+        maps[me, levels + l : levels + l + 1, :] = o[CHUNKS - 1 :]
+        before.append(
+            (jnp.where(sub == 0, 1.0, pltpu.roll(g, 1, 0)), jnp.where(sub == 0, 0.0, pltpu.roll(o, 1, 0)))
+        )
 
     def map_out(k):
         return remote(maps.at[me], maps.at[me], m_send.at[k], m_recv.at[k], k)
@@ -224,21 +259,25 @@
         growth = growth * own[:levels]
     wrap = offset / (1.0 - growth)
     inflow = prior_growth * wrap + prior_offset
-    spread = jnp.transpose(jnp.concatenate([inflow] * (LANES // levels), axis=0))
-
     areas = jnp.broadcast_to(area[...], (levels, rows))
     row = lane_index((levels, rows))
     masked = polar & (row >= row0) & (row < row0 + POLAR)
     part[lat, :levels] = jnp.where(masked, 0.0, areas * wrap)
     part[lat, levels:] = areas
 
-    for l in range(levels):
-        for first in range(0, rows, CHUNK):
-            part_rows = pl.ds(first, CHUNK)
-            level_inflow = jnp.broadcast_to(spread[first : first + CHUNK, l : l + 1], (CHUNK, LANES))
-            for h in range(halves):
-                c = pl.ds(h * LANES, LANES)
-                updated[l, part_rows, c] = cov[l, part_rows, c] * level_inflow + trv[l, part_rows, c]
+    inflows = jnp.stack([before[l][0] * inflow[l : l + 1] + before[l][1] for l in range(levels)])
+
+    def apply(v, carry):
+        ct[:, pl.ds(v, CHUNKS, stride=steps), :] = gs[v] * inflows + os[v]
+        return carry
+
+    lax.fori_loop(0, steps, apply, 0, unroll=4)
+
+    @pl.loop(0, levels)
+    def _(l):
+        for h in range(halves):
+            c = pl.ds(h * LANES, LANES)
+            updated[l, :, c] = jnp.transpose(ct[l, c, :])
 
     def part_out(k):
         return remote(part.at[lat], part.at[lat], d_send.at[k], d_recv.at[k], k, "lat")
@@ -299,37 +338,43 @@
     vmem = pl.BlockSpec(memory_space=pltpu.VMEM)
     hbm = pl.BlockSpec(memory_space=pl.ANY)
     dma = pltpu.SemaphoreType.DMA
+    inputs = (tracer, courant, hop_counts.reshape(1, rows), row_area.reshape(1, rows))
     updated, dateline = pl.pallas_call(
         functools.partial(kernel, n, z),
         out_shape=(
-            jax.ShapeDtypeStruct(tracer.shape, f32),
-            jax.ShapeDtypeStruct((1, levels), f32),
+            pltpu.VMEM(tracer.shape, f32),
+            pltpu.VMEM((1, levels), f32),
         ),
-        in_specs=[hbm, hbm, vmem, vmem],
+        in_specs=[hbm] * 4,
         out_specs=(vmem, vmem),
         scratch_shapes=[
             pltpu.VMEM(tracer.shape, f32),
             pltpu.VMEM(tracer.shape, f32),
-            pltpu.VMEM((rows, LANES), f32),
+            pltpu.VMEM((levels, cells, rows), f32),
+            pltpu.VMEM((levels, cells, rows), f32),
+            pltpu.VMEM((cells // CHUNKS, levels, CHUNKS, rows), f32),
+            pltpu.VMEM((cells // CHUNKS, levels, CHUNKS, rows), f32),
             pltpu.VMEM((n, 2 * levels, rows), f32),
             pltpu.VMEM((n, POLAR, cells), f32),
             pltpu.VMEM((n, POLAR, cells), f32),
             pltpu.VMEM((n, 2 * POLAR, cells), f32),
             pltpu.VMEM((levels, 2 * POLAR, cells), f32),
             pltpu.VMEM((z, 2 * levels, rows), f32),
-            dma((2, levels)), dma((2,)),
+            pltpu.VMEM((1, rows), jnp.int32),
+            pltpu.VMEM((1, rows), f32),
+            dma((2,)), dma((2, levels)), dma((2,)),
             dma((2, n)), dma((2, n)),
             dma((n,)), dma((n,)),
             dma((n,)), dma((n,)),
             dma((z,)), dma((z,)),
         ],
         compiler_params=pltpu.CompilerParams(
-            collective_id=0, has_side_effects=True, vmem_limit_bytes=16 * 1024 * 1024
+            collective_id=0, has_side_effects=True, vmem_limit_bytes=24 * 1024 * 1024
         ),
         cost_estimate=pl.CostEstimate(
             flops=60 * tracer.size, bytes_accessed=12 * tracer.size, transcendentals=tracer.size
         ),
-    )(tracer, courant, hop_counts.reshape(1, rows), row_area.reshape(1, rows))
+    )(*(pltpu.with_memory_space_constraint(a, pltpu.HBM) for a in inputs))
     return updated, dateline.reshape(levels)
 
 

time: 28.4 us -> 20.5 us (0.72)
  Pallas kernels: 22.9 us -> 18.2 us
  local copies, waits for them, and re-layouts: 4.59 us -> 1.48 us
    pallas_call x1, Pallas kernels: 22.9 us -> 18.2 us  [body(): pl.pallas_call(functools.partial(kernel, n, z), out_shape=(pltpu.VMEM(tra...]
    unnamed x10 -> x2, local copies, waits for them, and re-layouts: 4.59 us -> 1.48 us
where the time goes in v2:
time: 20.5 us; the launch traced here: 20.3 us
  Pallas kernels  18.2 us (89%)
  local copies, waits for them, and re-layouts  1.48 us (7%)
  between operations  0.64 us (3%)
    pallas_call x1, Pallas kernels, body(): pl.pallas_call(functools.partial(kernel, n, z), out_shape=(pltpu.VMEM(tra...  18.2 us
    unnamed x2, local copies, waits for them, and re-layouts  1.48 us

profile of v2, /device:TPU:0, one launch (start us, length us, event | category | flops | bytes accessed | tf_op | source)
XLA Modules:
  0.0 20.3 jit_solution(1790944932107872207)
XLA Ops:
  0.6 18.2 %shard_map.59 = (f32[8,128,256]{2,1,0:T(8,128)S(1)}, f32[1,8]{1,0:T(1,128)S(1)}) custom-call(f32[8,128,256]{2,1,0:T(8,128)} %tracer.1, f32[8,128,256]{2,1,0:T(8,128)} %courant.1, s32[1,128]{1,0:T(1,128)} %bitcast.4, f32[1,128]{1,0:T(1,128)} %bitcast.5), custom_call_target="tpu_custom_call" | custom-call | flops 15728640 | bytes 3145728 | tf_op jit(solution)/shard_map/pallas_call | solution.py:342
  18.8 1.0 %copy.8 = f32[8,128,256]{2,1,0:T(8,128)} copy(f32[8,128,256]{2,1,0:T(8,128)S(1)} %get-tuple-element.6) | data formatting | bytes 2097152
  19.8 0.5 %copy.9 = f32[8]{0:T(128)} copy(f32[8]{0:T(128)S(1)} %bitcast.3) | data formatting | bytes 64

commit v3 on v2

--- a/solution.py
+++ b/solution.py
@@ -11,6 +11,7 @@
 STOPS = 7
 LANES = 128
 CHUNKS = 8
+GROUP = 2
 
 
 def lane_index(shape):
@@ -83,12 +84,13 @@
         )
 
     def load(l):
+        some = pl.ds(l, GROUP)
         return (
-            pltpu.make_async_copy(tracer.at[l], trv.at[l], in_sem.at[0, l]),
-            pltpu.make_async_copy(courant.at[l], cov.at[l], in_sem.at[1, l]),
-        )
-
-    for l in range(levels):
+            pltpu.make_async_copy(tracer.at[some], trv.at[some], in_sem.at[0, l]),
+            pltpu.make_async_copy(courant.at[some], cov.at[some], in_sem.at[1, l]),
+        )
+
+    for l in range(0, levels, GROUP):
         for copy in load(l):
             copy.start()
     small = (
@@ -134,37 +136,43 @@
                 copy.start()
         is_worker(me, own)
 
-    @pl.loop(0, levels)
-    def _(l):
-        for copy in load(l):
-            copy.wait()
+    steps = cells // CHUNKS
+
+    def turn(l):
         for h in range(halves):
             c = pl.ds(h * LANES, LANES)
-            ct[l, c, :] = jnp.transpose(cov[l, :, c])
-            st[l, c, :] = jnp.transpose(trv[l, :, c])
-
+            here = cov[l, :, c]
+            above = 1.0 + here
+            shared = 1.0 / (here * above)
+            ratio = 1.0 - shared * here
+            cov[l, :, c] = shared * above
+            ct[l, c, :] = jnp.transpose(ratio)
+            st[l, c, :] = jnp.transpose(ratio * trv[l, :, c])
+
+    def run(l):
+        growth = offset = None
+        for v in range(steps):
+            cells_v = pl.ds(v, CHUNKS, stride=steps)
+            ratio, source = ct[l, cells_v, :], st[l, cells_v, :]
+            growth = ratio if v == 0 else growth * ratio
+            offset = source if v == 0 else ratio * offset + source
+            gs[l, v] = growth
+            os[l, v] = offset
+        return growth, offset
+
+    growth, offset = [], []
+    for l in range(levels + 1):
+        if l < levels:
+            if l % GROUP == 0:
+                for copy in load(l):
+                    copy.wait()
+            turn(l)
+        if l > 0:
+            g, o = run(l - 1)
+            growth.append(g)
+            offset.append(o)
     for copy in small:
         copy.wait()
-    steps = cells // CHUNKS
-
-    def step(v, state):
-        growth, offset = state
-        cells_v = pl.ds(v, CHUNKS, stride=steps)
-        here, source = ct[:, cells_v, :], st[:, cells_v, :]
-        above = 1.0 + here
-        shared = 1.0 / (here * above)
-        ratio = 1.0 - shared * here
-        inverse = shared * above
-        growth = growth * ratio
-        offset = ratio * source + ratio * offset
-        gs[v] = growth * inverse
-        os[v] = offset * inverse
-        return growth, offset
-
-    shape = (levels, CHUNKS, rows)
-    growth, offset = lax.fori_loop(
-        0, steps, step, (jnp.ones(shape, jnp.float32), jnp.zeros(shape, jnp.float32)), unroll=4
-    )
     sub = lax.broadcasted_iota(jnp.int32, (CHUNKS, rows), 0)
     before = []
     for l in range(levels):
@@ -265,19 +273,13 @@
     part[lat, :levels] = jnp.where(masked, 0.0, areas * wrap)
     part[lat, levels:] = areas
 
-    inflows = jnp.stack([before[l][0] * inflow[l : l + 1] + before[l][1] for l in range(levels)])
-
-    def apply(v, carry):
-        ct[:, pl.ds(v, CHUNKS, stride=steps), :] = gs[v] * inflows + os[v]
-        return carry
-
-    lax.fori_loop(0, steps, apply, 0, unroll=4)
-
-    @pl.loop(0, levels)
-    def _(l):
+    for l in range(levels):
+        entry = before[l][0] * inflow[l : l + 1] + before[l][1]
+        for v in range(steps):
+            ct[l, pl.ds(v, CHUNKS, stride=steps), :] = gs[l, v] * entry + os[l, v]
         for h in range(halves):
             c = pl.ds(h * LANES, LANES)
-            updated[l, :, c] = jnp.transpose(ct[l, c, :])
+            updated[l, :, c] = jnp.transpose(ct[l, c, :]) * cov[l, :, c]
 
     def part_out(k):
         return remote(part.at[lat], part.at[lat], d_send.at[k], d_recv.at[k], k, "lat")
@@ -330,6 +332,17 @@
             for k in range(1, n):
                 back_out(k).wait_send()
         is_worker(me, returned)
+
+
+def write_out(updated_in, dateline_in, updated, dateline, sem):
+    copies = (
+        pltpu.make_async_copy(updated_in, updated, sem.at[0]),
+        pltpu.make_async_copy(dateline_in, dateline, sem.at[1]),
+    )
+    for copy in copies:
+        copy.start()
+    for copy in copies:
+        copy.wait()
 
 
 def body(n, z, tracer, courant, hop_counts, row_area):
@@ -352,8 +365,8 @@
             pltpu.VMEM(tracer.shape, f32),
             pltpu.VMEM((levels, cells, rows), f32),
             pltpu.VMEM((levels, cells, rows), f32),
-            pltpu.VMEM((cells // CHUNKS, levels, CHUNKS, rows), f32),
-            pltpu.VMEM((cells // CHUNKS, levels, CHUNKS, rows), f32),
+            pltpu.VMEM((levels, cells // CHUNKS, CHUNKS, rows), f32),
+            pltpu.VMEM((levels, cells // CHUNKS, CHUNKS, rows), f32),
             pltpu.VMEM((n, 2 * levels, rows), f32),
             pltpu.VMEM((n, POLAR, cells), f32),
             pltpu.VMEM((n, POLAR, cells), f32),
@@ -375,6 +388,14 @@
             flops=60 * tracer.size, bytes_accessed=12 * tracer.size, transcendentals=tracer.size
         ),
     )(*(pltpu.with_memory_space_constraint(a, pltpu.HBM) for a in inputs))
+    held = (pltpu.with_memory_space_constraint(a, pltpu.VMEM) for a in (updated, dateline))
+    updated, dateline = pl.pallas_call(
+        write_out,
+        out_shape=(pltpu.HBM(tracer.shape, f32), pltpu.HBM((1, levels), f32)),
+        in_specs=[hbm, hbm],
+        out_specs=(hbm, hbm),
+        scratch_shapes=[dma((2,))],
+    )(*held)
     return updated, dateline.reshape(levels)
 
 

time: 20.5 us -> 20 us (0.976)
  local copies, waits for them, and re-layouts: 1.48 us -> 0 us
  Pallas kernels: 18.2 us -> 19.2 us
    unnamed x2 -> x0, local copies, waits for them, and re-layouts: 1.48 us -> none
    pallas_call x0 -> x1, Pallas kernels: none -> 0.99 us  [body(): pl.pallas_call(write_out, out_shape=(pltpu.HBM(tracer.shape, f32), pltpu....]
where the time goes in v3:
time: 20 us; the launch traced here: 19.8 us
  Pallas kernels  19.2 us (96%)
  between operations  0.64 us (3%)
    pallas_call x1, Pallas kernels, body(): pl.pallas_call(functools.partial(kernel, n, z), out_shape=(pltpu.VMEM(tra...  18.2 us
    pallas_call x1, Pallas kernels, body(): pl.pallas_call(write_out, out_shape=(pltpu.HBM(tracer.shape, f32), pltpu....  0.99 us

profile of v3, /device:TPU:0, one launch (start us, length us, event | category | flops | bytes accessed | tf_op | source)
XLA Modules:
  0.0 19.8 jit_solution(7813808607670028611)
XLA Ops:
  0.6 18.2 %shard_map.59 = (f32[8,128,256]{2,1,0:T(8,128)S(1)}, f32[1,8]{1,0:T(1,128)S(1)}) custom-call(f32[8,128,256]{2,1,0:T(8,128)} %tracer.1, f32[8,128,256]{2,1,0:T(8,128)} %courant.1, s32[1,128]{1,0:T(1,128)} %bitcast.3, f32[1,128]{1,0:T(1,128)} %bitcast.4), custom_call_target="tpu_custom_call" | custom-call | flops 15728640 | bytes 3145728 | tf_op jit(solution)/shard_map/pallas_call | solution.py:355
  18.8 1.0 %shard_map.60 = (f32[8,128,256]{2,1,0:T(8,128)}, f32[1,8]{1,0:T(1,128)}) custom-call(f32[8,128,256]{2,1,0:T(8,128)S(1)} %get-tuple-element.6.updated_in, f32[1,8]{1,0:T(1,128)S(1)} %get-tuple-element.7.dateline_in), custom_call_target="tpu_custom_call" | custom-call | tf_op jit(solution)/shard_map/pallas_call | solution.py:392

commit v4 on v3

v4 whole, which is shorter than its diff:
```python
import functools

import jax
import jax.numpy as jnp
from jax import lax
from jax.experimental import pallas as pl
from jax.experimental.pallas import tpu as pltpu
from jax.sharding import PartitionSpec as P

POLAR = 8
STOPS = 7
LANES = 128
CHUNKS = 8
GROUP = 2


def lane_index(shape):
    return lax.broadcasted_iota(jnp.int32, shape, len(shape) - 1)


def scan_lanes(growth, offset):
    lane = lane_index(growth.shape)
    stride = 1
    while stride < LANES:
        inside = lane >= stride
        lead_growth = pltpu.roll(growth, stride, 1)
        lead_offset = pltpu.roll(offset, stride, 1)
        offset = jnp.where(inside, growth * lead_offset + offset, offset)
        growth = jnp.where(inside, growth * lead_growth, growth)
        stride *= 2
    return growth, offset


def solve_block(courants, sources):
    out, end = [], None
    for courant, source in zip(courants, sources):
        above = 1.0 + courant
        shared = 1.0 / (courant * above)
        ratio = 1.0 - shared * courant
        inverse = shared * above
        growth, offset = scan_lanes(ratio, ratio * source)
        if end is not None:
            offset = growth * end[1] + offset
            growth = growth * end[0]
        end = (
            jnp.broadcast_to(growth[:, LANES - 1 :], growth.shape),
            jnp.broadcast_to(offset[:, LANES - 1 :], offset.shape),
        )
        out.append((growth * inverse, offset * inverse))
    return out, end


def kernel(
    n, z, tracer, courant, hops_in, area_in, updated, dateline,
    trv, cov, st, ct, gs, os, bg, bo, entry, maps, slabs, pin, pu, back, part, hops, area,
    small_sem, in_sem, slab_sem, p_sem, m_sem, b_sem, d_sem,
):
    levels, rows, cells = trv.shape
    halves = cells // LANES
    steps = cells // CHUNKS
    me = lax.axis_index("lon")
    lat = lax.axis_index("lat")
    polar = (lat == 0) | (lat == z - 1)
    row0 = pl.multiple_of(jnp.where(lat == 0, 0, rows - POLAR), POLAR)
    slab = pl.ds(row0, POLAR)
    own_level = lax.rem(me, levels)
    every = n == levels
    peers = n - 1 if every else levels - jnp.where(me < levels, 1, 0)

    def ahead(k):
        return lax.rem(me + k, n)

    def is_worker(device, work):
        if every:
            work()
        else:
            pl.when(device < levels)(work)

    barrier = pltpu.get_barrier_semaphore()
    for k in range(1, n):
        pl.semaphore_signal(barrier, inc=1, device_id={"lon": ahead(k)}, device_id_type=pl.DeviceIdType.MESH)
    for k in range(1, z):
        pl.semaphore_signal(
            barrier, inc=1, device_id={"lat": lax.rem(lat + k, z)}, device_id_type=pl.DeviceIdType.MESH
        )

    def load_slabs():
        return (
            pltpu.make_async_copy(courant.at[:, slab], slabs.at[:, 0], slab_sem.at[0]),
            pltpu.make_async_copy(tracer.at[:, slab], slabs.at[:, 1], slab_sem.at[1]),
        )

    @pl.when(polar)
    def _():
        for copy in load_slabs():
            copy.start()

    def load(l):
        some = pl.ds(l, GROUP)
        return (
            pltpu.make_async_copy(tracer.at[some], trv.at[some], in_sem.at[0, l]),
            pltpu.make_async_copy(courant.at[some], cov.at[some], in_sem.at[1, l]),
        )

    for l in range(0, levels, GROUP):
        for copy in load(l):
            copy.start()
    small = (
        pltpu.make_async_copy(hops_in, hops, small_sem.at[0]),
        pltpu.make_async_copy(area_in, area, small_sem.at[1]),
    )
    for copy in small:
        copy.start()

    def send(source, target, sem, k, axis="lon"):
        place = ahead(k) if axis == "lon" else lax.rem(lat + k, z)
        pltpu.make_async_remote_copy(
            src_ref=source, dst_ref=target, send_sem=sem.at[0], recv_sem=sem.at[1],
            device_id={axis: place}, device_id_type=pl.DeviceIdType.MESH,
        ).start()

    def wait(slots, sem, count):
        if isinstance(count, int):
            some = slots.at[pl.ds(0, count)]
            pltpu.make_async_copy(some, some, sem).wait()
        else:
            @pl.loop(0, count)
            def _(_):
                pltpu.make_async_copy(slots.at[0], slots.at[0], sem).wait()

    pl.semaphore_wait(barrier, n + z - 2)

    @pl.when(polar)
    def _():
        for copy in load_slabs():
            copy.wait()
        for k in range(1, n):
            is_worker(ahead(k), lambda k=k: send(slabs.at[lax.rem(ahead(k), levels)], pin.at[me], p_sem, k))
        pin[me] = slabs[own_level]

    @pl.loop(0, levels, step=GROUP)
    def _(first):
        for copy in load(first):
            copy.wait()
        for l in range(GROUP):
            for h in range(halves):
                c = pl.ds(h * LANES, LANES)
                here = cov[first + l, :, c]
                above = 1.0 + here
                shared = 1.0 / (here * above)
                ratio = 1.0 - shared * here
                cov[first + l, :, c] = shared * above
                ct[first + l, c, :] = jnp.transpose(ratio)
                st[first + l, c, :] = jnp.transpose(ratio * trv[first + l, :, c])

    def step(v, state):
        growth, offset = state
        cells_v = pl.ds(v, CHUNKS, stride=steps)
        ratio = ct[:, cells_v, :]
        growth = growth * ratio
        offset = ratio * offset + st[:, cells_v, :]
        gs[v] = growth
        os[v] = offset
        return growth, offset

    shape = (levels, CHUNKS, rows)
    growth, offset = lax.fori_loop(
        0, steps, step, (jnp.ones(shape, jnp.float32), jnp.zeros(shape, jnp.float32)), unroll=4
    )
    for copy in small:
        copy.wait()
    sub = lax.broadcasted_iota(jnp.int32, (CHUNKS, rows), 0)
    for l in range(levels):
        g, o = growth[l], offset[l]
        stride = 1
        while stride < CHUNKS:
            inside = sub >= stride
            lead_g, lead_o = pltpu.roll(g, stride, 0), pltpu.roll(o, stride, 0)
            o = jnp.where(inside, g * lead_o + o, o)
            g = jnp.where(inside, g * lead_g, g)
            stride *= 2
        maps[me, l : l + 1, :] = g[CHUNKS - 1 :]
        maps[me, levels + l : levels + l + 1, :] = o[CHUNKS - 1 :]
        bg[l] = jnp.where(sub == 0, 1.0, pltpu.roll(g, 1, 0))
        bo[l] = jnp.where(sub == 0, 0.0, pltpu.roll(o, 1, 0))

    for k in range(1, n):
        send(maps.at[me], maps.at[me], m_sem, k)

    def column(values):
        place = lane_index((POLAR, rows)) == lax.broadcasted_iota(jnp.int32, (POLAR, rows), 0) + row0
        return jnp.sum(jnp.where(place, jnp.broadcast_to(values, (POLAR, rows)), 0.0), axis=1, keepdims=True)

    def solve_polar():
        count = jnp.broadcast_to(column(hops[...].astype(jnp.float32)), (POLAR, LANES)).astype(jnp.int32)
        weights = column(area[...])
        wait(pin, p_sem.at[1], n - 1)
        courants, sources = [], []
        for h in range(halves):
            c = pl.ds(h * LANES, LANES)
            blocks = [pin[s, 1, :, c] for s in range(n)]
            for bit in range(STOPS.bit_length()):
                chosen = jnp.right_shift(count, bit) % 2 == 1
                blocks = [
                    jnp.where(chosen, blocks[(s - (1 << bit)) % n], blocks[s]) for s in range(n)
                ]
            sources.append(jnp.concatenate(blocks, axis=0))
            courants.append(jnp.concatenate([pin[s, 0, :, c] for s in range(n)], axis=0))
        out, end = solve_block(courants, sources)
        growth = jnp.ones((POLAR, LANES), jnp.float32)
        offset = jnp.zeros((POLAR, LANES), jnp.float32)
        prior = []
        for s in range(n):
            prior.append((growth, offset))
            own = slice(s * POLAR, (s + 1) * POLAR)
            offset = end[0][own] * offset + end[1][own]
            growth = growth * end[0][own]
        wrap = offset / (1.0 - growth)
        weighted = jnp.broadcast_to(jnp.sum(weights * wrap, axis=0, keepdims=True), (POLAR, LANES))
        for s in range(n):
            inflow = prior[s][0] * wrap + prior[s][1]
            own = slice(s * POLAR, (s + 1) * POLAR)
            for h, (g, o) in enumerate(out):
                c = pl.ds(h * LANES, LANES)
                pu[s, :POLAR, c] = g[own] * inflow + o[own]
                pu[s, POLAR:, c] = weighted
        for k in range(1, n):
            send(pu.at[ahead(k)], back.at[own_level], b_sem, k)
        back[own_level] = pu[me]

    @pl.when(polar)
    def _():
        is_worker(me, solve_polar)

    wait(maps, m_sem.at[1], n - 1)
    growth = jnp.ones((levels, rows), jnp.float32)
    offset = jnp.zeros((levels, rows), jnp.float32)
    prior_growth, prior_offset = growth, offset
    for s in range(n):
        here = s == me
        prior_growth = jnp.where(here, growth, prior_growth)
        prior_offset = jnp.where(here, offset, prior_offset)
        own = maps[s]
        offset = own[:levels] * offset + own[levels:]
        growth = growth * own[:levels]
    wrap = offset / (1.0 - growth)
    entry[...] = prior_growth * wrap + prior_offset

    areas = jnp.broadcast_to(area[...], (levels, rows))
    row = lane_index((levels, rows))
    masked = polar & (row >= row0) & (row < row0 + POLAR)
    part[lat, :levels] = jnp.where(masked, 0.0, areas * wrap)
    part[lat, levels:] = areas

    def write(low, high):
        @pl.loop(low, high, step=GROUP)
        def _(first):
            for l in range(GROUP):
                flow = bg[first + l] * entry[pl.ds(first + l, 1), :] + bo[first + l]
                for v in range(steps):
                    ct[first + l, pl.ds(v, CHUNKS, stride=steps), :] = gs[v, first + l] * flow + os[v, first + l]
                for h in range(halves):
                    c = pl.ds(h * LANES, LANES)
                    updated[first + l, :, c] = jnp.transpose(ct[first + l, c, :]) * cov[first + l, :, c]

    middle = levels // 2
    write(0, middle)

    @pl.when(polar)
    def _():
        wait(back, b_sem.at[1], peers)
        total = jnp.zeros((levels, LANES), jnp.float32)
        sub = lax.broadcasted_iota(jnp.int32, (levels, LANES), 0)
        for l in range(levels):
            total = jnp.where(sub == l, back[l, POLAR : POLAR + 1, :LANES], total)
        first_lane = lane_index((levels, LANES)) == 0
        part[lat, :levels, :LANES] = part[lat, :levels, :LANES] + jnp.where(first_lane, total, 0.0)

    for k in range(1, z):
        send(part.at[lat], part.at[lat], d_sem, k, "lat")

    write(middle, levels)

    @pl.when(polar)
    def _():
        for l in range(levels):
            updated[l, slab, :] = back[l, :POLAR, :]
        wait(slabs, p_sem.at[0], peers)
        is_worker(me, lambda: wait(pu, b_sem.at[0], n - 1))

    wait(maps, m_sem.at[0], n - 1)
    wait(part, d_sem.at[0], z - 1)
    wait(part, d_sem.at[1], z - 1)
    total = part[0]
    for s in range(1, z):
        total = total + part[s]
    sums = jnp.sum(total, axis=1, keepdims=True)
    mean = jnp.broadcast_to(sums[:levels] / sums[levels:], (levels, LANES))
    diagonal = lax.broadcasted_iota(jnp.int32, (levels, LANES), 0) == lane_index((levels, LANES))
    dateline[...] = jnp.sum(jnp.where(diagonal, mean, 0.0), axis=0, keepdims=True)[:, :levels]


def write_out(updated_in, dateline_in, updated, dateline, sem):
    copies = (
        pltpu.make_async_copy(updated_in, updated, sem.at[0]),
        pltpu.make_async_copy(dateline_in, dateline, sem.at[1]),
    )
    for copy in copies:
        copy.start()
    for copy in copies:
        copy.wait()


def body(n, z, tracer, courant, hop_counts, row_area):
    levels, rows, cells = tracer.shape
    f32 = jnp.float32
    vmem = pl.BlockSpec(memory_space=pltpu.VMEM)
    hbm = pl.BlockSpec(memory_space=pl.ANY)
    dma = pltpu.SemaphoreType.DMA
    inputs = (tracer, courant, hop_counts.reshape(1, rows), row_area.reshape(1, rows))
    updated, dateline = pl.pallas_call(
        functools.partial(kernel, n, z),
        out_shape=(
            pltpu.VMEM(tracer.shape, f32),
            pltpu.VMEM((1, levels), f32),
        ),
        in_specs=[hbm] * 4,
        out_specs=(vmem, vmem),
        scratch_shapes=[
            pltpu.VMEM(tracer.shape, f32),
            pltpu.VMEM(tracer.shape, f32),
            pltpu.VMEM((levels, cells, rows), f32),
            pltpu.VMEM((levels, cells, rows), f32),
            pltpu.VMEM((cells // CHUNKS, levels, CHUNKS, rows), f32),
            pltpu.VMEM((cells // CHUNKS, levels, CHUNKS, rows), f32),
            pltpu.VMEM((levels, CHUNKS, rows), f32),
            pltpu.VMEM((levels, CHUNKS, rows), f32),
            pltpu.VMEM((levels, rows), f32),
            pltpu.VMEM((n, 2 * levels, rows), f32),
            pltpu.VMEM((levels, 2, POLAR, cells), f32),
            pltpu.VMEM((n, 2, POLAR, cells), f32),
            pltpu.VMEM((n, 2 * POLAR, cells), f32),
            pltpu.VMEM((levels, 2 * POLAR, cells), f32),
            pltpu.VMEM((z, 2 * levels, rows), f32),
            pltpu.VMEM((1, rows), jnp.int32),
            pltpu.VMEM((1, rows), f32),
            dma((2,)), dma((2, levels)), dma((2,)),
            dma((2,)), dma((2,)), dma((2,)), dma((2,)),
        ],
        compiler_params=pltpu.CompilerParams(
            collective_id=0, has_side_effects=True, vmem_limit_bytes=24 * 1024 * 1024
        ),
        cost_estimate=pl.CostEstimate(
            flops=60 * tracer.size, bytes_accessed=12 * tracer.size, transcendentals=tracer.size
        ),
    )(*(pltpu.with_memory_space_constraint(a, pltpu.HBM) for a in inputs))
    held = (pltpu.with_memory_space_constraint(a, pltpu.VMEM) for a in (updated, dateline))
    updated, dateline = pl.pallas_call(
        write_out,
        out_shape=(pltpu.HBM(tracer.shape, f32), pltpu.HBM((1, levels), f32)),
        in_specs=[hbm, hbm],
        out_specs=(hbm, hbm),
        scratch_shapes=[dma((2,))],
    )(*held)
    return updated, dateline.reshape(levels)


def solution(mesh):
    return jax.shard_map(
        functools.partial(body, mesh.shape["lon"], mesh.shape["lat"]),
        mesh=mesh,
        in_specs=(P(None, "lat", "lon"), P(None, "lat", "lon"), P("lat"), P("lat")),
        out_specs=(P(None, "lat", "lon"), P()),
        check_vma=False,
    )
```

time: 20 us -> 19 us (0.950)
  Pallas kernels: 19.2 us -> 18.2 us
    pallas_call x1, Pallas kernels: 18.2 us -> 17.2 us  [body(): pl.pallas_call(functools.partial(kernel, n, z), out_shape=(pltpu.VMEM(tra...]
where the time goes in v4:
time: 19 us; the launch traced here: 18.9 us
  Pallas kernels  18.2 us (96%)
  between operations  0.64 us (3%)
    pallas_call x1, Pallas kernels, body(): pl.pallas_call(functools.partial(kernel, n, z), out_shape=(pltpu.VMEM(tra...  17.2 us
    pallas_call x1, Pallas kernels, body(): pl.pallas_call(write_out, out_shape=(pltpu.HBM(tracer.shape, f32), pltpu....  0.99 us

profile of v4, /device:TPU:0, one launch (start us, length us, event | category | flops | bytes accessed | tf_op | source)
XLA Modules:
  0.0 18.9 jit_solution(7513414669639422027)
XLA Ops:
  0.6 17.2 %shard_map.59 = (f32[8,128,256]{2,1,0:T(8,128)S(1)}, f32[1,8]{1,0:T(1,128)S(1)}) custom-call(f32[8,128,256]{2,1,0:T(8,128)} %tracer.1, f32[8,128,256]{2,1,0:T(8,128)} %courant.1, s32[1,128]{1,0:T(1,128)} %bitcast.3, f32[1,128]{1,0:T(1,128)} %bitcast.4), custom_call_target="tpu_custom_call" | custom-call | flops 15728640 | bytes 3145728 | tf_op jit(solution)/shard_map/pallas_call | solution.py:321
  17.9 1.0 %shard_map.60 = (f32[8,128,256]{2,1,0:T(8,128)}, f32[1,8]{1,0:T(1,128)}) custom-call(f32[8,128,256]{2,1,0:T(8,128)S(1)} %get-tuple-element.6.updated_in, f32[1,8]{1,0:T(1,128)S(1)} %get-tuple-element.7.dateline_in), custom_call_target="tpu_custom_call" | custom-call | tf_op jit(solution)/shard_map/pallas_call | solution.py:358

commit v5 on v4

--- a/solution.py
+++ b/solution.py
@@ -77,9 +77,13 @@
             pl.when(device < levels)(work)
 
     barrier = pltpu.get_barrier_semaphore()
-    for k in range(1, n):
+
+    @pl.loop(1, n)
+    def _(k):
         pl.semaphore_signal(barrier, inc=1, device_id={"lon": ahead(k)}, device_id_type=pl.DeviceIdType.MESH)
-    for k in range(1, z):
+
+    @pl.loop(1, z)
+    def _(k):
         pl.semaphore_signal(
             barrier, inc=1, device_id={"lat": lax.rem(lat + k, z)}, device_id_type=pl.DeviceIdType.MESH
         )
@@ -134,8 +138,11 @@
     def _():
         for copy in load_slabs():
             copy.wait()
-        for k in range(1, n):
-            is_worker(ahead(k), lambda k=k: send(slabs.at[lax.rem(ahead(k), levels)], pin.at[me], p_sem, k))
+
+        @pl.loop(1, n)
+        def _(k):
+            is_worker(ahead(k), lambda: send(slabs.at[lax.rem(ahead(k), levels)], pin.at[me], p_sem, k))
+
         pin[me] = slabs[own_level]
 
     @pl.loop(0, levels, step=GROUP)
@@ -184,7 +191,8 @@
         bg[l] = jnp.where(sub == 0, 1.0, pltpu.roll(g, 1, 0))
         bo[l] = jnp.where(sub == 0, 0.0, pltpu.roll(o, 1, 0))
 
-    for k in range(1, n):
+    @pl.loop(1, n)
+    def _(k):
         send(maps.at[me], maps.at[me], m_sem, k)
 
     def column(values):
@@ -224,8 +232,11 @@
                 c = pl.ds(h * LANES, LANES)
                 pu[s, :POLAR, c] = g[own] * inflow + o[own]
                 pu[s, POLAR:, c] = weighted
-        for k in range(1, n):
+
+        @pl.loop(1, n)
+        def _(k):
             send(pu.at[ahead(k)], back.at[own_level], b_sem, k)
+
         back[own_level] = pu[me]
 
     @pl.when(polar)
@@ -252,22 +263,7 @@
     part[lat, :levels] = jnp.where(masked, 0.0, areas * wrap)
     part[lat, levels:] = areas
 
-    def write(low, high):
-        @pl.loop(low, high, step=GROUP)
-        def _(first):
-            for l in range(GROUP):
-                flow = bg[first + l] * entry[pl.ds(first + l, 1), :] + bo[first + l]
-                for v in range(steps):
-                    ct[first + l, pl.ds(v, CHUNKS, stride=steps), :] = gs[v, first + l] * flow + os[v, first + l]
-                for h in range(halves):
-                    c = pl.ds(h * LANES, LANES)
-                    updated[first + l, :, c] = jnp.transpose(ct[first + l, c, :]) * cov[first + l, :, c]
-
-    middle = levels // 2
-    write(0, middle)
-
-    @pl.when(polar)
-    def _():
+    def take_back():
         wait(back, b_sem.at[1], peers)
         total = jnp.zeros((levels, LANES), jnp.float32)
         sub = lax.broadcasted_iota(jnp.int32, (levels, LANES), 0)
@@ -276,10 +272,25 @@
         first_lane = lane_index((levels, LANES)) == 0
         part[lat, :levels, :LANES] = part[lat, :levels, :LANES] + jnp.where(first_lane, total, 0.0)
 
-    for k in range(1, z):
-        send(part.at[lat], part.at[lat], d_sem, k, "lat")
-
-    write(middle, levels)
+    middle = levels // 2 // GROUP * GROUP
+
+    @pl.loop(0, levels, step=GROUP)
+    def _(first):
+        @pl.when(first == middle)
+        def _():
+            pl.when(polar)(take_back)
+
+            @pl.loop(1, z)
+            def _(k):
+                send(part.at[lat], part.at[lat], d_sem, k, "lat")
+
+        for l in range(GROUP):
+            flow = bg[first + l] * entry[pl.ds(first + l, 1), :] + bo[first + l]
+            for v in range(steps):
+                ct[first + l, pl.ds(v, CHUNKS, stride=steps), :] = gs[v, first + l] * flow + os[v, first + l]
+            for h in range(halves):
+                c = pl.ds(h * LANES, LANES)
+                updated[first + l, :, c] = jnp.transpose(ct[first + l, c, :]) * cov[first + l, :, c]
 
     @pl.when(polar)
     def _():
@@ -301,10 +312,9 @@
 
 
 def write_out(updated_in, dateline_in, updated, dateline, sem):
-    copies = (
-        pltpu.make_async_copy(updated_in, updated, sem.at[0]),
-        pltpu.make_async_copy(dateline_in, dateline, sem.at[1]),
-    )
+    levels = updated.shape[0]
+    copies = [pltpu.make_async_copy(updated_in.at[l], updated.at[l], sem.at[l]) for l in range(levels)]
+    copies.append(pltpu.make_async_copy(dateline_in, dateline, sem.at[levels]))
     for copy in copies:
         copy.start()
     for copy in copies:
@@ -360,7 +370,7 @@
         out_shape=(pltpu.HBM(tracer.shape, f32), pltpu.HBM((1, levels), f32)),
         in_specs=[hbm, hbm],
         out_specs=(hbm, hbm),
-        scratch_shapes=[dma((2,))],
+        scratch_shapes=[dma((levels + 1,))],
     )(*held)
     return updated, dateline.reshape(levels)
 

time: 19 us -> 19.1 us (level)
  no operation moved by 1% of the time
where the time goes in v5:
time: 19.1 us; the launch traced here: 18.9 us
  Pallas kernels  18.3 us (96%)
  between operations  0.64 us (3%)
    pallas_call x1, Pallas kernels, body(): pl.pallas_call(functools.partial(kernel, n, z), out_shape=(pltpu.VMEM(tra...  17.3 us
    pallas_call x1, Pallas kernels, body(): pl.pallas_call(write_out, out_shape=(pltpu.HBM(tracer.shape, f32), pltpu....  1.04 us

profile of v5, /device:TPU:0, one launch (start us, length us, event | category | flops | bytes accessed | tf_op | source)
XLA Modules:
  0.0 18.9 jit_solution(16349315886485435797)
XLA Ops:
  0.6 17.3 %shard_map.59 = (f32[8,128,256]{2,1,0:T(8,128)S(1)}, f32[1,8]{1,0:T(1,128)S(1)}) custom-call(f32[8,128,256]{2,1,0:T(8,128)} %tracer.1, f32[8,128,256]{2,1,0:T(8,128)} %courant.1, s32[1,128]{1,0:T(1,128)} %bitcast.3, f32[1,128]{1,0:T(1,128)} %bitcast.4), custom_call_target="tpu_custom_call" | custom-call | flops 15728640 | bytes 3145728 | tf_op jit(solution)/shard_map/pallas_call | solution.py:331
  17.9 1.0 %shard_map.60 = (f32[8,128,256]{2,1,0:T(8,128)}, f32[1,8]{1,0:T(1,128)}) custom-call(f32[8,128,256]{2,1,0:T(8,128)S(1)} %get-tuple-element.6.updated_in, f32[1,8]{1,0:T(1,128)S(1)} %get-tuple-element.7.dateline_in), custom_call_target="tpu_custom_call" | custom-call | tf_op jit(solution)/shard_map/pallas_call | solution.py:368

commit v6 on v5

--- a/solution.py
+++ b/solution.py
@@ -12,6 +12,7 @@
 LANES = 128
 CHUNKS = 8
 GROUP = 2
+EARLY = 4
 
 
 def lane_index(shape):
@@ -132,21 +133,7 @@
             def _(_):
                 pltpu.make_async_copy(slots.at[0], slots.at[0], sem).wait()
 
-    pl.semaphore_wait(barrier, n + z - 2)
-
-    @pl.when(polar)
-    def _():
-        for copy in load_slabs():
-            copy.wait()
-
-        @pl.loop(1, n)
-        def _(k):
-            is_worker(ahead(k), lambda: send(slabs.at[lax.rem(ahead(k), levels)], pin.at[me], p_sem, k))
-
-        pin[me] = slabs[own_level]
-
-    @pl.loop(0, levels, step=GROUP)
-    def _(first):
+    def turn(first):
         for copy in load(first):
             copy.wait()
         for l in range(GROUP):
@@ -159,6 +146,24 @@
                 cov[first + l, :, c] = shared * above
                 ct[first + l, c, :] = jnp.transpose(ratio)
                 st[first + l, c, :] = jnp.transpose(ratio * trv[first + l, :, c])
+
+    early = levels * EARLY // 8 // GROUP * GROUP
+    pl.loop(0, early, step=GROUP)(turn)
+
+    pl.semaphore_wait(barrier, n + z - 2)
+
+    @pl.when(polar)
+    def _():
+        for copy in load_slabs():
+            copy.wait()
+
+        @pl.loop(1, n)
+        def _(k):
+            is_worker(ahead(k), lambda: send(slabs.at[lax.rem(ahead(k), levels)], pin.at[me], p_sem, k))
+
+        pin[me] = slabs[own_level]
+
+    pl.loop(early, levels, step=GROUP)(turn)
 
     def step(v, state):
         growth, offset = state
@@ -312,9 +317,10 @@
 
 
 def write_out(updated_in, dateline_in, updated, dateline, sem):
-    levels = updated.shape[0]
-    copies = [pltpu.make_async_copy(updated_in.at[l], updated.at[l], sem.at[l]) for l in range(levels)]
-    copies.append(pltpu.make_async_copy(dateline_in, dateline, sem.at[levels]))
+    copies = (
+        pltpu.make_async_copy(updated_in, updated, sem.at[0]),
+        pltpu.make_async_copy(dateline_in, dateline, sem.at[1]),
+    )
     for copy in copies:
         copy.start()
     for copy in copies:
@@ -370,7 +376,7 @@
         out_shape=(pltpu.HBM(tracer.shape, f32), pltpu.HBM((1, levels), f32)),
         in_specs=[hbm, hbm],
         out_specs=(hbm, hbm),
-        scratch_shapes=[dma((levels + 1,))],
+        scratch_shapes=[dma((2,))],
     )(*held)
     return updated, dateline.reshape(levels)
 

time: 19.1 us -> 19 us (level)
  no operation moved by 1% of the time
where the time goes in v6:
time: 19 us; the launch traced here: 18.9 us
  Pallas kernels  18.2 us (96%)
  between operations  0.64 us (3%)
    pallas_call x1, Pallas kernels, body(): pl.pallas_call(functools.partial(kernel, n, z), out_shape=(pltpu.VMEM(tra...  17.3 us
    pallas_call x1, Pallas kernels, body(): pl.pallas_call(write_out, out_shape=(pltpu.HBM(tracer.shape, f32), pltpu....  0.99 us

profile of v6, /device:TPU:0, one launch (start us, length us, event | category | flops | bytes accessed | tf_op | source)
XLA Modules:
  0.0 18.9 jit_solution(11267407686962185646)
XLA Ops:
  0.6 17.3 %shard_map.59 = (f32[8,128,256]{2,1,0:T(8,128)S(1)}, f32[1,8]{1,0:T(1,128)S(1)}) custom-call(f32[8,128,256]{2,1,0:T(8,128)} %tracer.1, f32[8,128,256]{2,1,0:T(8,128)} %courant.1, s32[1,128]{1,0:T(1,128)} %bitcast.3, f32[1,128]{1,0:T(1,128)} %bitcast.4), custom_call_target="tpu_custom_call" | custom-call | flops 15728640 | bytes 3145728 | tf_op jit(solution)/shard_map/pallas_call | solution.py:337
  17.9 1.0 %shard_map.60 = (f32[8,128,256]{2,1,0:T(8,128)}, f32[1,8]{1,0:T(1,128)}) custom-call(f32[8,128,256]{2,1,0:T(8,128)S(1)} %get-tuple-element.6.updated_in, f32[1,8]{1,0:T(1,128)S(1)} %get-tuple-element.7.dateline_in), custom_call_target="tpu_custom_call" | custom-call | tf_op jit(solution)/shard_map/pallas_call | solution.py:374

commit v7 on v6

--- a/solution.py
+++ b/solution.py
@@ -53,7 +53,7 @@
 
 def kernel(
     n, z, tracer, courant, hops_in, area_in, updated, dateline,
-    trv, cov, st, ct, gs, os, bg, bo, entry, maps, slabs, pin, pu, back, part, hops, area,
+    trv, cov, order, st, ct, gs, os, bg, bo, entry, maps, slabs, pin, pu, back, part, hops, area,
     small_sem, in_sem, slab_sem, p_sem, m_sem, b_sem, d_sem,
 ):
     levels, rows, cells = trv.shape
@@ -133,19 +133,32 @@
             def _(_):
                 pltpu.make_async_copy(slots.at[0], slots.at[0], sem).wait()
 
+    place = lax.broadcasted_iota(jnp.int32, (cells, cells), 0)
+    target = (place % CHUNKS) * steps + place // CHUNKS
+    order[...] = jnp.where(lane_index((cells, cells)) == target, 1.0, 0.0).astype(jnp.bfloat16)
+
+    def reorder(values):
+        parts = []
+        for _ in range(3):
+            parts.append(values.astype(jnp.bfloat16))
+            values = values - parts[-1].astype(jnp.float32)
+        return lax.dot_general(
+            jnp.concatenate([order[...]] * 3, axis=1), jnp.concatenate(parts, axis=1),
+            (((1,), (1,)), ((), ())), preferred_element_type=jnp.float32,
+        )
+
     def turn(first):
         for copy in load(first):
             copy.wait()
         for l in range(GROUP):
-            for h in range(halves):
-                c = pl.ds(h * LANES, LANES)
-                here = cov[first + l, :, c]
-                above = 1.0 + here
-                shared = 1.0 / (here * above)
-                ratio = 1.0 - shared * here
-                cov[first + l, :, c] = shared * above
-                ct[first + l, c, :] = jnp.transpose(ratio)
-                st[first + l, c, :] = jnp.transpose(ratio * trv[first + l, :, c])
+            here = cov[first + l]
+            above = 1.0 + here
+            shared = 1.0 / (here * above)
+            ratio = 1.0 - shared * here
+            cov[first + l] = shared * above
+            both = reorder(jnp.concatenate([ratio, ratio * trv[first + l]], axis=0))
+            ct[first + l] = both[:, :rows]
+            st[first + l] = both[:, rows:]
 
     early = levels * EARLY // 8 // GROUP * GROUP
     pl.loop(0, early, step=GROUP)(turn)
@@ -167,7 +180,7 @@
 
     def step(v, state):
         growth, offset = state
-        cells_v = pl.ds(v, CHUNKS, stride=steps)
+        cells_v = pl.ds(pl.multiple_of(v * CHUNKS, CHUNKS), CHUNKS)
         ratio = ct[:, cells_v, :]
         growth = growth * ratio
         offset = ratio * offset + st[:, cells_v, :]
@@ -277,17 +290,19 @@
         first_lane = lane_index((levels, LANES)) == 0
         part[lat, :levels, :LANES] = part[lat, :levels, :LANES] + jnp.where(first_lane, total, 0.0)
 
-    middle = levels // 2 // GROUP * GROUP
+    def send_part():
+        @pl.loop(1, z)
+        def _(k):
+            send(part.at[lat], part.at[lat], d_sem, k, "lat")
+
+    pl.when(jnp.logical_not(polar))(send_part)
 
     @pl.loop(0, levels, step=GROUP)
     def _(first):
-        @pl.when(first == middle)
+        @pl.when(polar & (first == GROUP))
         def _():
-            pl.when(polar)(take_back)
-
-            @pl.loop(1, z)
-            def _(k):
-                send(part.at[lat], part.at[lat], d_sem, k, "lat")
+            take_back()
+            send_part()
 
         for l in range(GROUP):
             flow = bg[first + l] * entry[pl.ds(first + l, 1), :] + bo[first + l]
@@ -345,6 +360,7 @@
         scratch_shapes=[
             pltpu.VMEM(tracer.shape, f32),
             pltpu.VMEM(tracer.shape, f32),
+            pltpu.VMEM((cells, cells), jnp.bfloat16),
             pltpu.VMEM((levels, cells, rows), f32),
             pltpu.VMEM((levels, cells, rows), f32),
             pltpu.VMEM((cells // CHUNKS, levels, CHUNKS, rows), f32),

time: 19 us -> 19.5 us (1.026)
  Pallas kernels: 18.2 us -> 18.7 us
    pallas_call x1, Pallas kernels: 17.3 us -> 17.7 us  [body(): pl.pallas_call(functools.partial(kernel, n, z), out_shape=(pltpu.VMEM(tra...]
where the time goes in v7:
time: 19.5 us; the launch traced here: 19.4 us
  Pallas kernels  18.7 us (96%)
  between operations  0.64 us (3%)
    pallas_call x1, Pallas kernels, body(): pl.pallas_call(functools.partial(kernel, n, z), out_shape=(pltpu.VMEM(tra...  17.7 us
    pallas_call x1, Pallas kernels, body(): pl.pallas_call(write_out, out_shape=(pltpu.HBM(tracer.shape, f32), pltpu....  0.99 us

profile of v7, /device:TPU:0, one launch (start us, length us, event | category | flops | bytes accessed | tf_op | source)
XLA Modules:
  0.0 19.4 jit_solution(7229408205556157403)
XLA Ops:
  0.6 17.7 %shard_map.59 = (f32[8,128,256]{2,1,0:T(8,128)S(1)}, f32[1,8]{1,0:T(1,128)S(1)}) custom-call(f32[8,128,256]{2,1,0:T(8,128)} %tracer.1, f32[8,128,256]{2,1,0:T(8,128)} %courant.1, s32[1,128]{1,0:T(1,128)} %bitcast.3, f32[1,128]{1,0:T(1,128)} %bitcast.4), custom_call_target="tpu_custom_call" | custom-call | flops 15728640 | bytes 3145728 | tf_op jit(solution)/shard_map/pallas_call | solution.py:352
  18.4 1.0 %shard_map.60 = (f32[8,128,256]{2,1,0:T(8,128)}, f32[1,8]{1,0:T(1,128)}) custom-call(f32[8,128,256]{2,1,0:T(8,128)S(1)} %get-tuple-element.6.updated_in, f32[1,8]{1,0:T(1,128)S(1)} %get-tuple-element.7.dateline_in), custom_call_target="tpu_custom_call" | custom-call | tf_op jit(solution)/shard_map/pallas_call | solution.py:390

commit v8 on v6

--- a/solution.py
+++ b/solution.py
@@ -12,7 +12,7 @@
 LANES = 128
 CHUNKS = 8
 GROUP = 2
-EARLY = 4
+EARLY = 2
 
 
 def lane_index(shape):
@@ -182,6 +182,7 @@
     for copy in small:
         copy.wait()
     sub = lax.broadcasted_iota(jnp.int32, (CHUNKS, rows), 0)
+    whole = []
     for l in range(levels):
         g, o = growth[l], offset[l]
         stride = 1
@@ -193,12 +194,15 @@
             stride *= 2
         maps[me, l : l + 1, :] = g[CHUNKS - 1 :]
         maps[me, levels + l : levels + l + 1, :] = o[CHUNKS - 1 :]
-        bg[l] = jnp.where(sub == 0, 1.0, pltpu.roll(g, 1, 0))
-        bo[l] = jnp.where(sub == 0, 0.0, pltpu.roll(o, 1, 0))
+        whole.append((g, o))
 
     @pl.loop(1, n)
     def _(k):
         send(maps.at[me], maps.at[me], m_sem, k)
+
+    for l, (g, o) in enumerate(whole):
+        bg[l] = jnp.where(sub == 0, 1.0, pltpu.roll(g, 1, 0))
+        bo[l] = jnp.where(sub == 0, 0.0, pltpu.roll(o, 1, 0))
 
     def column(values):
         place = lane_index((POLAR, rows)) == lax.broadcasted_iota(jnp.int32, (POLAR, rows), 0) + row0
@@ -277,17 +281,19 @@
         first_lane = lane_index((levels, LANES)) == 0
         part[lat, :levels, :LANES] = part[lat, :levels, :LANES] + jnp.where(first_lane, total, 0.0)
 
-    middle = levels // 2 // GROUP * GROUP
+    def send_part():
+        @pl.loop(1, z)
+        def _(k):
+            send(part.at[lat], part.at[lat], d_sem, k, "lat")
+
+    pl.when(jnp.logical_not(polar))(send_part)
 
     @pl.loop(0, levels, step=GROUP)
     def _(first):
-        @pl.when(first == middle)
+        @pl.when(polar & (first == GROUP))
         def _():
-            pl.when(polar)(take_back)
-
-            @pl.loop(1, z)
-            def _(k):
-                send(part.at[lat], part.at[lat], d_sem, k, "lat")
+            take_back()
+            send_part()
 
         for l in range(GROUP):
             flow = bg[first + l] * entry[pl.ds(first + l, 1), :] + bo[first + l]

time: 19 us -> 19 us (level)
  no operation moved by 1% of the time
where the time goes in v8:
time: 19 us; the launch traced here: 18.9 us
  Pallas kernels  18.2 us (96%)
  between operations  0.64 us (3%)
    pallas_call x1, Pallas kernels, body(): pl.pallas_call(functools.partial(kernel, n, z), out_shape=(pltpu.VMEM(tra...  17.3 us
    pallas_call x1, Pallas kernels, body(): pl.pallas_call(write_out, out_shape=(pltpu.HBM(tracer.shape, f32), pltpu....  0.99 us

profile of v8, /device:TPU:0, one launch (start us, length us, event | category | flops | bytes accessed | tf_op | source)
XLA Modules:
  0.0 18.9 jit_solution(6745257320052173605)
XLA Ops:
  0.6 17.3 %shard_map.59 = (f32[8,128,256]{2,1,0:T(8,128)S(1)}, f32[1,8]{1,0:T(1,128)S(1)}) custom-call(f32[8,128,256]{2,1,0:T(8,128)} %tracer.1, f32[8,128,256]{2,1,0:T(8,128)} %courant.1, s32[1,128]{1,0:T(1,128)} %bitcast.3, f32[1,128]{1,0:T(1,128)} %bitcast.4), custom_call_target="tpu_custom_call" | custom-call | flops 15728640 | bytes 3145728 | tf_op jit(solution)/shard_map/pallas_call | solution.py:343
  17.9 1.0 %shard_map.60 = (f32[8,128,256]{2,1,0:T(8,128)}, f32[1,8]{1,0:T(1,128)}) custom-call(f32[8,128,256]{2,1,0:T(8,128)S(1)} %get-tuple-element.6.updated_in, f32[1,8]{1,0:T(1,128)S(1)} %get-tuple-element.7.dateline_in), custom_call_target="tpu_custom_call" | custom-call | tf_op jit(solution)/shard_map/pallas_call | solution.py:380

commit v9 on v8

--- a/solution.py
+++ b/solution.py
@@ -238,9 +238,8 @@
             inflow = prior[s][0] * wrap + prior[s][1]
             own = slice(s * POLAR, (s + 1) * POLAR)
             for h, (g, o) in enumerate(out):
-                c = pl.ds(h * LANES, LANES)
-                pu[s, :POLAR, c] = g[own] * inflow + o[own]
-                pu[s, POLAR:, c] = weighted
+                pu[s, h * POLAR : (h + 1) * POLAR, :] = g[own] * inflow + o[own]
+            pu[s, halves * POLAR :, :] = weighted
 
         @pl.loop(1, n)
         def _(k):
@@ -277,7 +276,7 @@
         total = jnp.zeros((levels, LANES), jnp.float32)
         sub = lax.broadcasted_iota(jnp.int32, (levels, LANES), 0)
         for l in range(levels):
-            total = jnp.where(sub == l, back[l, POLAR : POLAR + 1, :LANES], total)
+            total = jnp.where(sub == l, back[l, halves * POLAR : halves * POLAR + 1, :], total)
         first_lane = lane_index((levels, LANES)) == 0
         part[lat, :levels, :LANES] = part[lat, :levels, :LANES] + jnp.where(first_lane, total, 0.0)
 
@@ -306,7 +305,8 @@
     @pl.when(polar)
     def _():
         for l in range(levels):
-            updated[l, slab, :] = back[l, :POLAR, :]
+            for h in range(halves):
+                updated[l, slab, pl.ds(h * LANES, LANES)] = back[l, h * POLAR : (h + 1) * POLAR, :]
         wait(slabs, p_sem.at[0], peers)
         is_worker(me, lambda: wait(pu, b_sem.at[0], n - 1))
 
@@ -361,8 +361,8 @@
             pltpu.VMEM((n, 2 * levels, rows), f32),
             pltpu.VMEM((levels, 2, POLAR, cells), f32),
             pltpu.VMEM((n, 2, POLAR, cells), f32),
-            pltpu.VMEM((n, 2 * POLAR, cells), f32),
-            pltpu.VMEM((levels, 2 * POLAR, cells), f32),
+            pltpu.VMEM((n, (cells // LANES + 1) * POLAR, LANES), f32),
+            pltpu.VMEM((levels, (cells // LANES + 1) * POLAR, LANES), f32),
             pltpu.VMEM((z, 2 * levels, rows), f32),
             pltpu.VMEM((1, rows), jnp.int32),
             pltpu.VMEM((1, rows), f32),

time: 19 us -> 18.9 us (level)
  no operation moved by 1% of the time
where the time goes in v9:
time: 18.9 us; the launch traced here: 18.7 us
  Pallas kernels  18.1 us (96%)
  between operations  0.64 us (3%)
    pallas_call x1, Pallas kernels, body(): pl.pallas_call(functools.partial(kernel, n, z), out_shape=(pltpu.VMEM(tra...  17.1 us
    pallas_call x1, Pallas kernels, body(): pl.pallas_call(write_out, out_shape=(pltpu.HBM(tracer.shape, f32), pltpu....  0.99 us

profile of v9, /device:TPU:0, one launch (start us, length us, event | category | flops | bytes accessed | tf_op | source)
XLA Modules:
  0.0 18.7 jit_solution(3073006021832551409)
XLA Ops:
  0.6 17.1 %shard_map.59 = (f32[8,128,256]{2,1,0:T(8,128)S(1)}, f32[1,8]{1,0:T(1,128)S(1)}) custom-call(f32[8,128,256]{2,1,0:T(8,128)} %tracer.1, f32[8,128,256]{2,1,0:T(8,128)} %courant.1, s32[1,128]{1,0:T(1,128)} %bitcast.3, f32[1,128]{1,0:T(1,128)} %bitcast.4), custom_call_target="tpu_custom_call" | custom-call | flops 15728640 | bytes 3145728 | tf_op jit(solution)/shard_map/pallas_call | solution.py:343
  17.7 1.0 %shard_map.60 = (f32[8,128,256]{2,1,0:T(8,128)}, f32[1,8]{1,0:T(1,128)}) custom-call(f32[8,128,256]{2,1,0:T(8,128)S(1)} %get-tuple-element.6.updated_in, f32[1,8]{1,0:T(1,128)S(1)} %get-tuple-element.7.dateline_in), custom_call_target="tpu_custom_call" | custom-call | tf_op jit(solution)/shard_map/pallas_call | solution.py:380

commit v10 on v9

--- a/solution.py
+++ b/solution.py
@@ -165,44 +165,8 @@
 
     pl.loop(early, levels, step=GROUP)(turn)
 
-    def step(v, state):
-        growth, offset = state
-        cells_v = pl.ds(v, CHUNKS, stride=steps)
-        ratio = ct[:, cells_v, :]
-        growth = growth * ratio
-        offset = ratio * offset + st[:, cells_v, :]
-        gs[v] = growth
-        os[v] = offset
-        return growth, offset
-
-    shape = (levels, CHUNKS, rows)
-    growth, offset = lax.fori_loop(
-        0, steps, step, (jnp.ones(shape, jnp.float32), jnp.zeros(shape, jnp.float32)), unroll=4
-    )
     for copy in small:
         copy.wait()
-    sub = lax.broadcasted_iota(jnp.int32, (CHUNKS, rows), 0)
-    whole = []
-    for l in range(levels):
-        g, o = growth[l], offset[l]
-        stride = 1
-        while stride < CHUNKS:
-            inside = sub >= stride
-            lead_g, lead_o = pltpu.roll(g, stride, 0), pltpu.roll(o, stride, 0)
-            o = jnp.where(inside, g * lead_o + o, o)
-            g = jnp.where(inside, g * lead_g, g)
-            stride *= 2
-        maps[me, l : l + 1, :] = g[CHUNKS - 1 :]
-        maps[me, levels + l : levels + l + 1, :] = o[CHUNKS - 1 :]
-        whole.append((g, o))
-
-    @pl.loop(1, n)
-    def _(k):
-        send(maps.at[me], maps.at[me], m_sem, k)
-
-    for l, (g, o) in enumerate(whole):
-        bg[l] = jnp.where(sub == 0, 1.0, pltpu.roll(g, 1, 0))
-        bo[l] = jnp.where(sub == 0, 0.0, pltpu.roll(o, 1, 0))
 
     def column(values):
         place = lane_index((POLAR, rows)) == lax.broadcasted_iota(jnp.int32, (POLAR, rows), 0) + row0
@@ -250,6 +214,43 @@
     @pl.when(polar)
     def _():
         is_worker(me, solve_polar)
+
+    def step(v, state):
+        growth, offset = state
+        cells_v = pl.ds(v, CHUNKS, stride=steps)
+        ratio = ct[:, cells_v, :]
+        growth = growth * ratio
+        offset = ratio * offset + st[:, cells_v, :]
+        gs[v] = growth
+        os[v] = offset
+        return growth, offset
+
+    shape = (levels, CHUNKS, rows)
+    growth, offset = lax.fori_loop(
+        0, steps, step, (jnp.ones(shape, jnp.float32), jnp.zeros(shape, jnp.float32)), unroll=4
+    )
+    sub = lax.broadcasted_iota(jnp.int32, (CHUNKS, rows), 0)
+    whole = []
+    for l in range(levels):
+        g, o = growth[l], offset[l]
+        stride = 1
+        while stride < CHUNKS:
+            inside = sub >= stride
+            lead_g, lead_o = pltpu.roll(g, stride, 0), pltpu.roll(o, stride, 0)
+            o = jnp.where(inside, g * lead_o + o, o)
+            g = jnp.where(inside, g * lead_g, g)
+            stride *= 2
+        maps[me, l : l + 1, :] = g[CHUNKS - 1 :]
+        maps[me, levels + l : levels + l + 1, :] = o[CHUNKS - 1 :]
+        whole.append((g, o))
+
+    @pl.loop(1, n)
+    def _(k):
+        send(maps.at[me], maps.at[me], m_sem, k)
+
+    for l, (g, o) in enumerate(whole):
+        bg[l] = jnp.where(sub == 0, 1.0, pltpu.roll(g, 1, 0))
+        bo[l] = jnp.where(sub == 0, 0.0, pltpu.roll(o, 1, 0))
 
     wait(maps, m_sem.at[1], n - 1)
     growth = jnp.ones((levels, rows), jnp.float32)

time: 18.9 us -> 21.2 us (1.12)
  Pallas kernels: 18.1 us -> 20.4 us
    pallas_call x1, Pallas kernels: 17.1 us -> 19.4 us  [body(): pl.pallas_call(functools.partial(kernel, n, z), out_shape=(pltpu.VMEM(tra...]
where the time goes in v10:
time: 21.2 us; the launch traced here: 21 us
  Pallas kernels  20.4 us (96%)
  between operations  0.64 us (3%)
    pallas_call x1, Pallas kernels, body(): pl.pallas_call(functools.partial(kernel, n, z), out_shape=(pltpu.VMEM(tra...  19.4 us
    pallas_call x1, Pallas kernels, body(): pl.pallas_call(write_out, out_shape=(pltpu.HBM(tracer.shape, f32), pltpu....  0.99 us

profile of v10, /device:TPU:0, one launch (start us, length us, event | category | flops | bytes accessed | tf_op | source)
XLA Modules:
  0.0 21.0 jit_solution(11466883124164390388)
XLA Ops:
  0.6 19.4 %shard_map.59 = (f32[8,128,256]{2,1,0:T(8,128)S(1)}, f32[1,8]{1,0:T(1,128)S(1)}) custom-call(f32[8,128,256]{2,1,0:T(8,128)} %tracer.1, f32[8,128,256]{2,1,0:T(8,128)} %courant.1, s32[1,128]{1,0:T(1,128)} %bitcast.3, f32[1,128]{1,0:T(1,128)} %bitcast.4), custom_call_target="tpu_custom_call" | custom-call | flops 15728640 | bytes 3145728 | tf_op jit(solution)/shard_map/pallas_call | solution.py:344
  20.1 1.0 %shard_map.60 = (f32[8,128,256]{2,1,0:T(8,128)}, f32[1,8]{1,0:T(1,128)}) custom-call(f32[8,128,256]{2,1,0:T(8,128)S(1)} %get-tuple-element.6.updated_in, f32[1,8]{1,0:T(1,128)S(1)} %get-tuple-element.7.dateline_in), custom_call_target="tpu_custom_call" | custom-call | tf_op jit(solution)/shard_map/pallas_call | solution.py:381
